TPU v7x, 512 devices: a whole 4x4x16 slice. The times are simulated.
512 devices in a mesh: row: 4 (over x), rad: 16 (over z), ax: 8 (over y, core).
Axes of the slice: x: 4, y: 4, z: 16, core: 2. Of those that a mesh axis runs over, the one named last changes fastest.
Arguments:
- state: float32 [7, 4, 128, 64, 128], P(None, 'row', 'rad', 'ax'), may hold values from -6 to 6
- axial_speed: float32 [4, 128, 64, 128], P('row', 'rad', 'ax'), may hold values from 0.3 to 1
- viscosity: float32 [4, 128, 64, 128], P('row', 'rad', 'ax'), may hold values from 0.02 to 0.1
- relaxation: float32 [7], replicated, may hold values from 0.05 to 0.5
- face_area: float32 [4, 128, 64], P('row', 'rad', 'ax'), may hold values from 1 to 10
- face_station: int32 [4, 128, 64], P('row', 'rad', 'ax'), may hold values from 0 to 127, as said below
- limiter_flags: int32 [4, 128, 64], P('row', 'rad', 'ax'), may hold values 0 or 1
- inlet_profile: float32 [7, 128], P(None, 'rad'), may hold values from -6 to 6
Outputs:
- new_state: float32 [7, 4, 128, 64, 128], P(None, 'row', 'rad', 'ax')
- outlet_profile: float32 [7, 4, 128], P(None, 'row', 'rad')
- outlet_pressure: float32 [4, 128], P('row', 'rad')
Inputs may be any that keep to these rules, and one draw needn't show every extreme that they name: `face_station`: a face cell at radial index i has a station in the aligned group of 8 stations that holds i, and at circumferential index 0 its station is i itself.
All inputs are finite; a program needn't handle non-finite values. No bound on the sum of `limiter_flags` on one device may be relied on, other than what follows from the above.
Results may differ from a plain program's by a relative error of at most 0.0003.
Values sent between devices are 32-bit elements; how exact they have to be, the bound alone decides.
A program may use at most 64 MiB of HBM per device.

v0:
```python
import jax
import jax.numpy as jnp
from jax import lax
from jax.sharding import PartitionSpec as P

SWEEPS = 4


pseudo_step = 0.5


def shifted_2(array, axis, by):
    count = lax.axis_size(axis)
    pairs = [(i, i + by) for i in range(count) if 0 <= i + by < count]
    return lax.ppermute(array, axis, pairs)


def extended_2(cells, sides, width, closed):
    for axis, dim in sides:
        count = lax.axis_size(axis)
        ends = count if closed else count - 1
        head = lax.slice_in_dim(cells, 0, width, axis=dim)
        tail = lax.slice_in_dim(cells, cells.shape[dim] - width, cells.shape[dim], axis=dim)
        cells = jnp.concatenate(
            [
                lax.ppermute(tail, axis, [(i, (i + 1) % count) for i in range(ends)]),
                cells,
                lax.ppermute(head, axis, [((i + 1) % count, i) for i in range(ends)]),
            ],
            axis=dim,
        )
    return cells


def limited_slope(first, second):
    return 0.5 * (jnp.sign(first) + jnp.sign(second)) * jnp.minimum(jnp.abs(first), jnp.abs(second))


def advance(
    field,
    inlet_ghost,
    outlet_ghost,
    radial_plus,
    radial_minus,
    pitch_plus,
    pitch_minus,
    axial_speed,
    viscosity,
    relax_column,
    flags,
):
    length = field.shape[-1]
    extended = jnp.concatenate(
        [inlet_ghost[..., None], inlet_ghost[..., None], field, outlet_ghost[..., None]], axis=-1
    )
    upwind_two = extended[..., 0 : length + 1]
    upwind_one = extended[..., 1 : length + 2]
    downwind = extended[..., 2 : length + 3]
    face_speed = jnp.concatenate([axial_speed[..., :1], axial_speed], axis=-1)
    left_state = upwind_one + 0.5 * flags[..., None] * limited_slope(
        upwind_one - upwind_two, downwind - upwind_one
    )
    face_flux = face_speed * left_state
    convection = face_flux[..., :-1] - face_flux[..., 1:]
    laplacian = (
        extended[..., 3 : length + 3]
        + extended[..., 1 : length + 1]
        + radial_plus
        + radial_minus
        + pitch_plus
        + pitch_minus
        - 6.0 * field
    )
    return field + pseudo_step * (convection + viscosity * laplacian - relax_column * field)


def body(
    state, axial_speed, viscosity, relaxation, face_area, face_station, limiter_flags, inlet_profile
):
    field = state[:, 0]
    variables = field.shape[0]
    radial_cells = field.shape[1]
    pitch_cells = field.shape[2]
    speed_local = axial_speed[0]
    visc_local = viscosity[0]
    flags = limiter_flags[0].astype(jnp.float32)
    weights = face_area[0].reshape(-1)
    stations_flat = face_station[0].reshape(-1)
    relax_column = relaxation[:, None, None, None]
    rad_index = lax.axis_index("rad")
    stations = radial_cells * lax.axis_size("rad")
    local_hot = (
        (stations_flat - rad_index * radial_cells)[:, None]
        == jnp.arange(radial_cells, dtype=jnp.int32)[None, :]
    ).astype(jnp.float32)
    scale_radial = 4.0 / stations
    profile = None
    pressure = None
    for sweep_index in range(SWEEPS):
        outlet_cells = field[..., -1]
        weighted = outlet_cells.reshape(variables, -1) * weights[None, :]
        whole_hot = (
            stations_flat[:, None] == jnp.arange(stations, dtype=jnp.int32)[None, :]
        ).astype(jnp.float32)
        numerator, denominator = lax.psum(
            (
                jnp.dot(weighted, whole_hot, precision=lax.Precision.HIGHEST),
                jnp.dot(weights, whole_hot, precision=lax.Precision.HIGHEST),
            ),
            ("rad", "ax"),
        )
        whole_profile = numerator / denominator[None]
        whole_radius = 1.0 + jnp.arange(stations, dtype=jnp.float32) / stations
        swirl_term = whole_profile[3] * whole_profile[3] / whole_radius
        whole_pressure = whole_profile[4] + scale_radial * (jnp.cumsum(swirl_term) - swirl_term)
        profile = lax.dynamic_slice_in_dim(whole_profile, rad_index * radial_cells, radial_cells, 1)
        pressure = lax.dynamic_slice_in_dim(
            whole_pressure, rad_index * radial_cells, radial_cells, 0
        )
        shifted = shifted_2(profile, "row", 1)
        upstream = jnp.where(lax.axis_index("row") == 0, inlet_profile, shifted)
        inlet_ghost = jnp.dot(upstream, local_hot.T, precision=lax.Precision.HIGHEST).reshape(
            variables, radial_cells, pitch_cells
        )
        pressure_cells = jnp.dot(pressure, local_hot.T, precision=lax.Precision.HIGHEST).reshape(
            radial_cells, pitch_cells
        )
        outlet_ghost = jnp.concatenate(
            [outlet_cells[:4], pressure_cells[None], outlet_cells[5:]], axis=0
        )
        radial_padded = extended_2(field, (("rad", 1),), 1, False)
        pitch_padded = extended_2(field, (("ax", 2),), 1, True)
        field = advance(
            field,
            inlet_ghost,
            outlet_ghost,
            radial_padded[:, 2:],
            radial_padded[:, :-2],
            pitch_padded[:, :, 2:],
            pitch_padded[:, :, :-2],
            speed_local,
            visc_local,
            relax_column,
            flags,
        )
    return (field[:, None], profile[:, None], pressure[None])


def solution(mesh):
    return jax.shard_map(
        body,
        mesh=mesh,
        in_specs=(
            P(None, "row", "rad", "ax", None),
            P("row", "rad", "ax", None),
            P("row", "rad", "ax", None),
            P(),
            P("row", "rad", "ax"),
            P("row", "rad", "ax"),
            P("row", "rad", "ax"),
            P(None, "rad"),
        ),
        out_specs=(P(None, "row", "rad", "ax", None), P(None, "row", "rad"), P("row", "rad")),
        check_vma=False,
    )
```

profile of v0, /device:TPU:409, one launch (start us, length us, event | category | flops | bytes accessed | tf_op | source)
XLA Modules:
  0.0 1072.0 jit_solution(14707224980680287648)
XLA Ops:
  0.6 0.8 mul.285
  1.6 0.7 copy-done.5
  2.3 1.2 slice_reduce_fusion.3
  4.0 235.7 %all-reduce = (f32[7,128]{1,0:T(8,128)S(1)}, f32[128]{0:T(128)S(1)}) all-reduce(f32[7,128]{1,0:T(8,128)S(1)} %fusion.72, f32[128]{0:T(128)S(1)} %convolution_bitcast_fusion), channel_id=1, replica_groups=mesh['row'=4,'rad'=16,'ax'=8] {'rad','ax'}, use_global_device_ids=true, to_apply=%region_0.0 | all-reduce | flops 1024 | bytes 8192 | tf_op jit(solution)/shard_map/psum | solution.py:105
  239.8 3.1 collective-permute-start
  242.9 18.5 %collective-permute-start.1 = (f32[7,1,8,128]{3,2,1,0:T(8,128)S(1)}, f32[7,1,8,128]{3,2,1,0:T(8,128)S(1)}, u32[]{:S(2)}, u32[]{:S(2)}) collective-permute-start(f32[7,1,8,128]{3,2,1,0:T(8,128)S(1)} %get-tuple-element.41), channel_id=1, source_target_pairs={{8,0},{16,8},{24,16},{32,24},{40,32},{48,40},{56,48},{64,56},{72,6... | collective-permute-start | bytes 86024 | tf_op jit(solution)/shard_map/ppermute | solution.py:28
  261.4 1.9 collective-permute-start.2
  263.4 5.5 collective-permute-start.4
  272.1 0.5 add_multiply_fusion.3
  272.6 0.8 collective-permute-done.3
  273.4 0.7 copy-done.4
  275.3 233.4 %psum.36 = f32[7,128]{1,0:T(8,128)S(1)} all-reduce(f32[7,128]{1,0:T(8,128)S(1)} %fusion.71), channel_id=1, replica_groups=mesh['row'=4,'rad'=16,'ax'=8] {'rad','ax'}, use_global_device_ids=true, to_apply=%region_3.4 | all-reduce | flops 896 | bytes 7168 | tf_op jit(solution)/shard_map/psum | solution.py:105
  508.9 3.1 collective-permute-start.5
  512.0 15.7 %collective-permute-start.6 = (f32[7,1,8,128]{3,2,1,0:T(8,128)S(1)}, f32[7,1,8,128]{3,2,1,0:T(8,128)S(1)}, u32[]{:S(2)}, u32[]{:S(2)}) collective-permute-start(f32[7,1,8,128]{3,2,1,0:T(8,128)S(1)} %get-tuple-element.37), channel_id=1, source_target_pairs={{8,0},{16,8},{24,16},{32,24},{40,32},{48,40},{56,48},{64,56},{72,6... | collective-permute-start | bytes 86024 | tf_op jit(solution)/shard_map/ppermute | solution.py:28
  527.7 1.9 collective-permute-start.7
  529.7 5.5 collective-permute-start.9
  537.3 2.4 collective-permute-done.8
  540.9 231.8 %psum.39 = f32[7,128]{1,0:T(8,128)S(1)} all-reduce(f32[7,128]{1,0:T(8,128)S(1)} %fusion.70), channel_id=1, replica_groups=mesh['row'=4,'rad'=16,'ax'=8] {'rad','ax'}, use_global_device_ids=true, to_apply=%region_5.6 | all-reduce | flops 896 | bytes 7168 | tf_op jit(solution)/shard_map/psum | solution.py:105
  772.9 2.8 collective-permute-start.10
  775.7 17.3 %collective-permute-start.11 = (f32[7,1,8,128]{3,2,1,0:T(8,128)S(1)}, f32[7,1,8,128]{3,2,1,0:T(8,128)S(1)}, u32[]{:S(2)}, u32[]{:S(2)}) collective-permute-start(f32[7,1,8,128]{3,2,1,0:T(8,128)S(1)} %get-tuple-element.33), channel_id=1, source_target_pairs={{8,0},{16,8},{24,16},{32,24},{40,32},{48,40},{56,48},{64,56},{72,6... | collective-permute-start | bytes 86024 | tf_op jit(solution)/shard_map/ppermute | solution.py:28
  793.0 1.9 collective-permute-start.12
  795.0 5.5 collective-permute-start.14
  802.6 2.4 collective-permute-done.13
  806.2 231.8 %psum.48 = f32[7,128]{1,0:T(8,128)S(1)} all-reduce(f32[7,128]{1,0:T(8,128)S(1)} %fusion.69), channel_id=1, replica_groups=mesh['row'=4,'rad'=16,'ax'=8] {'rad','ax'}, use_global_device_ids=true, to_apply=%region_7.8 | all-reduce | flops 896 | bytes 7168 | tf_op jit(solution)/shard_map/psum | solution.py:105
  1038.9 0.6 dynamic-slice_bitcast_fusion.6
  1039.5 0.6 copy.406
  1040.1 1.6 collective-permute-start.15
  1041.7 17.3 %collective-permute-start.16 = (f32[7,1,8,128]{3,2,1,0:T(8,128)S(1)}, f32[7,1,8,128]{3,2,1,0:T(8,128)S(1)}, u32[]{:S(2)}, u32[]{:S(2)}) collective-permute-start(f32[7,1,8,128]{3,2,1,0:T(8,128)S(1)} %get-tuple-element.29), channel_id=1, source_target_pairs={{8,0},{16,8},{24,16},{32,24},{40,32},{48,40},{56,48},{64,56},{72,6... | collective-permute-start | bytes 86024 | tf_op jit(solution)/shard_map/ppermute | solution.py:28
  1059.0 1.9 collective-permute-start.17
  1060.9 5.5 collective-permute-start.19
  1067.9 3.0 collective-permute-done.18
  1070.9 1.0 fusion.24
  (126 shorter events, 14.1 us)
Async XLA Ops:
  0.6 0.8 copy-start.3
  1.6 0.7 copy-start.5
  1.6 241.3 %copy-start = (f32[7,1,8,8,128]{4,3,2,1,0:T(8,128)S(1)}, f32[7,1,8,8,128]{4,3,2,1,0:T(8,128)}, u32[]{:S(2)}) copy-start(f32[7,1,8,8,128]{4,3,2,1,0:T(8,128)} %param.8) | copy-start | bytes 688132
  239.8 31.6 %collective-permute-start = (f32[7,8]{1,0:T(8,128)S(1)}, f32[7,8]{1,0:T(8,128)S(1)}, u32[]{:S(2)}, u32[]{:S(2)}) collective-permute-start(f32[7,8]{1,0:T(8,128)S(1)} %constant_dynamic-slice_fusion.3), channel_id=1, source_target_pairs={{0,128},{128,256},{256,384},{1,129},{129,257},{257,385},{2,130},{1... | collective-permute-start | bytes 680 | tf_op jit(solution)/shard_map/ppermute | solution.py:15
  242.9 29.7 %collective-permute-start.1 = (f32[7,1,8,128]{3,2,1,0:T(8,128)S(1)}, f32[7,1,8,128]{3,2,1,0:T(8,128)S(1)}, u32[]{:S(2)}, u32[]{:S(2)}) collective-permute-start(f32[7,1,8,128]{3,2,1,0:T(8,128)S(1)} %get-tuple-element.41), channel_id=1, source_target_pairs={{8,0},{16,8},{24,16},{32,24},{40,32},{48,40},{56,48},{64,56},{72,6... | collective-permute-start | bytes 86024 | tf_op jit(solution)/shard_map/ppermute | solution.py:28
  261.4 11.2 %collective-permute-start.2 = (f32[7,1,8,128]{3,2,1,0:T(8,128)S(1)}, f32[7,1,8,128]{3,2,1,0:T(8,128)S(1)}, u32[]{:S(2)}, u32[]{:S(2)}) collective-permute-start(f32[7,1,8,128]{3,2,1,0:T(8,128)S(1)} %get-tuple-element.42), channel_id=1, source_target_pairs={{0,8},{8,16},{16,24},{24,32},{32,40},{40,48},{48,56},{56,64},{64,7... | collective-permute-start | bytes 86024 | tf_op jit(solution)/shard_map/ppermute | solution.py:26
  263.4 9.2 collective-permute-start.4
  268.9 4.5 collective-permute-start.3
  269.1 0.7 copy-start.6
  270.1 0.8 copy-start.2
  270.9 0.7 copy-start.7
  272.0 1.4 copy-start.1
  273.4 0.7 copy-start.4
  508.9 27.4 %collective-permute-start.5 = (f32[7,8]{1,0:T(8,128)S(1)}, f32[7,8]{1,0:T(8,128)S(1)}, u32[]{:S(2)}, u32[]{:S(2)}) collective-permute-start(f32[7,8]{1,0:T(8,128)S(1)} %constant_dynamic-slice_fusion.2), channel_id=1, source_target_pairs={{0,128},{128,256},{256,384},{1,129},{129,257},{257,385},{2,130},{1... | collective-permute-start | bytes 680 | tf_op jit(solution)/shard_map/ppermute | solution.py:15
  512.0 25.2 %collective-permute-start.6 = (f32[7,1,8,128]{3,2,1,0:T(8,128)S(1)}, f32[7,1,8,128]{3,2,1,0:T(8,128)S(1)}, u32[]{:S(2)}, u32[]{:S(2)}) collective-permute-start(f32[7,1,8,128]{3,2,1,0:T(8,128)S(1)} %get-tuple-element.37), channel_id=1, source_target_pairs={{8,0},{16,8},{24,16},{32,24},{40,32},{48,40},{56,48},{64,56},{72,6... | collective-permute-start | bytes 86024 | tf_op jit(solution)/shard_map/ppermute | solution.py:28
  527.7 9.5 collective-permute-start.7
  529.7 7.6 collective-permute-start.9
  535.2 4.5 collective-permute-start.8
  772.9 28.7 %collective-permute-start.10 = (f32[7,8]{1,0:T(8,128)S(1)}, f32[7,8]{1,0:T(8,128)S(1)}, u32[]{:S(2)}, u32[]{:S(2)}) collective-permute-start(f32[7,8]{1,0:T(8,128)S(1)} %constant_dynamic-slice_fusion.1), channel_id=1, source_target_pairs={{0,128},{128,256},{256,384},{1,129},{129,257},{257,385},{2,130},{1... | collective-permute-start | bytes 680 | tf_op jit(solution)/shard_map/ppermute | solution.py:15
  775.7 26.8 %collective-permute-start.11 = (f32[7,1,8,128]{3,2,1,0:T(8,128)S(1)}, f32[7,1,8,128]{3,2,1,0:T(8,128)S(1)}, u32[]{:S(2)}, u32[]{:S(2)}) collective-permute-start(f32[7,1,8,128]{3,2,1,0:T(8,128)S(1)} %get-tuple-element.33), channel_id=1, source_target_pairs={{8,0},{16,8},{24,16},{32,24},{40,32},{48,40},{56,48},{64,56},{72,6... | collective-permute-start | bytes 86024 | tf_op jit(solution)/shard_map/ppermute | solution.py:28
  793.0 9.5 collective-permute-start.12
  795.0 7.6 collective-permute-start.14
  800.5 4.5 collective-permute-start.13
  1040.1 26.9 %collective-permute-start.15 = (f32[7,8]{1,0:T(8,128)S(1)}, f32[7,8]{1,0:T(8,128)S(1)}, u32[]{:S(2)}, u32[]{:S(2)}) collective-permute-start(f32[7,8]{1,0:T(8,128)S(1)} %constant_dynamic-slice_fusion), channel_id=1, source_target_pairs={{0,128},{128,256},{256,384},{1,129},{129,257},{257,385},{2,130},{1... | collective-permute-start | bytes 680 | tf_op jit(solution)/shard_map/ppermute | solution.py:15
  1041.7 26.2 %collective-permute-start.16 = (f32[7,1,8,128]{3,2,1,0:T(8,128)S(1)}, f32[7,1,8,128]{3,2,1,0:T(8,128)S(1)}, u32[]{:S(2)}, u32[]{:S(2)}) collective-permute-start(f32[7,1,8,128]{3,2,1,0:T(8,128)S(1)} %get-tuple-element.29), channel_id=1, source_target_pairs={{8,0},{16,8},{24,16},{32,24},{40,32},{48,40},{56,48},{64,56},{72,6... | collective-permute-start | bytes 86024 | tf_op jit(solution)/shard_map/ppermute | solution.py:28
  1059.0 8.9 collective-permute-start.17
  1060.9 7.0 collective-permute-start.19
  1066.4 4.5 collective-permute-start.18
where the time goes:
time: 1070 us
  blocking collectives  933 us (87%)
  starting transfers between devices  109 us (10%)
  local copies, waits for them, and re-layouts  12.1 us (1%)
    psum x4, blocking collectives, body(): lax.psum((jnp.dot(weighted, whole_hot, precision=lax.Precision.HIGHEST),...  933 us
    ppermute x8, starting transfers between devices, extended_2(): lax.ppermute(head, axis, [((i + 1) % count, i) for i in range(ends)])  68.8 us
    ppermute x8, starting transfers between devices, extended_2(): lax.ppermute(tail, axis, [(i, (i + 1) % count) for i in range(ends)])  29.7 us
  transfers between devices with their start and end apart: 20, of which 4 were waited for; matrix products, arithmetic and copies ran while one was open for 1% of the time, Pallas kernels for 0%

commit v1 on v0

v1 whole, which is shorter than its diff:
```python
import functools

import jax
import jax.numpy as jnp
from jax import lax
from jax.experimental import pallas as pl
from jax.experimental.pallas import tpu as pltpu
from jax.sharding import PartitionSpec as P

MESH = pl.DeviceIdType.MESH
SWEEPS = 4
NV = 7
PV = 4
SV = 3
RC = 8
CC = 8
NX = 128
REACH = 4


def kernel(
    sizes,
    state,
    speed,
    visc,
    relax,
    area,
    station,
    flags,
    inlet,
    out,
    out_profile,
    out_pressure,
    field,
    axs,
    axr,
    radr,
    ms_src,
    ms_own,
    ms_up,
    t_src,
    px,
    coef,
    weight,
    hot,
    upstream,
    inlet_t,
    ghosts,
    profile_s,
    s_ax,
    r_ax,
    s_rad,
    r_rad,
    s_own,
    r_own,
    s_down,
    r_up,
    s_px,
    r_px,
    ready,
):
    rows, rads, axes = sizes
    row, rad, ax = lax.axis_index("row"), lax.axis_index("rad"), lax.axis_index("ax")
    lane = lax.broadcasted_iota(jnp.int32, (8, NX), 1)
    sub = lax.broadcasted_iota(jnp.int32, (8, NX), 0)
    zero = jnp.zeros((8, NX), jnp.float32)

    def remote(src, dst, ssem, rsem, where):
        return pltpu.make_async_remote_copy(
            src_ref=src, dst_ref=dst, send_sem=ssem, recv_sem=rsem, device_id=where, device_id_type=MESH
        )

    barrier = pltpu.get_barrier_semaphore()

    def greet(where):
        pl.semaphore_signal(barrier, inc=1, device_id=where, device_id_type=MESH)

    for d in range(1, axes):
        greet({"ax": lax.rem(ax + d, axes)})

    @pl.when(rad > 0)
    def _():
        greet({"rad": rad - 1})

    for d in range(1, REACH + 1):

        @pl.when(rad + d < rads)
        def _():
            greet({"rad": rad + d})

    @pl.when(row > 0)
    def _():
        for d in range(axes):
            greet({"row": row - 1, "ax": d})

    @pl.when(rad == 0)
    def _():
        radr[:, 0] = jnp.zeros_like(radr[:, 0])

    @pl.when(rad == rads - 1)
    def _():
        radr[:, 1] = jnp.zeros_like(radr[:, 1])

    for d in range(1, REACH + 1):

        @pl.when(rad < d)
        def _():
            px[:, d - 1] = jnp.zeros_like(px[:, d - 1])

    diagonal = sub == lane

    def column(ref, r):
        wide = jnp.broadcast_to(ref[r : r + 1, :], (8, 8))
        return jnp.sum(jnp.where(diagonal[:, :8], wide, 0.0), axis=1, keepdims=True)

    areas = area[...]
    local_station = (station[...] - rad * RC).astype(jnp.float32)
    flag = flags[...].astype(jnp.float32)
    for r in range(RC):
        st = jnp.broadcast_to(column(local_station, r), (8, NX))
        ar = jnp.broadcast_to(column(areas, r), (8, NX))
        hot[r] = st
        for s in range(RC):
            weight[s, r] = jnp.where(st == float(s), ar, 0.0)
        a = 0.5 * speed[r]
        coef[0, r] = a
        coef[1, r] = a * (0.5 * jnp.broadcast_to(column(flag, r), (8, NX)))
        coef[2, r] = 0.5 * visc[r]
    turned = zero
    inlet_all = inlet[...]
    for v in range(NV):
        turned = jnp.where(lane == v, column(inlet_all, v), turned)
    inlet_t[...] = turned

    def sums(picks, p):
        total = zero
        for s in range(RC):
            acc = weight[s, 0] * picks[0]
            for r in range(1, RC):
                acc = acc + weight[s, r] * picks[r]
            total = jnp.where(sub == s, jnp.sum(acc, axis=0, keepdims=True), total)
        ms_src[p] = total
        ms_own[p, ax] = total

    def pack(src, p, v):
        for r in range(RC):
            axs[p, 0, v, r : r + 1, :] = src[v, r, 0:1, :]
            axs[p, 1, v, r : r + 1, :] = src[v, r, CC - 1 : CC, :]

    def tail(x):
        return jnp.broadcast_to(x[:, NX - 1 : NX], (8, NX))

    def first(v, picks):
        pack(state, 0, v)
        return tuple(jnp.where(lane == v, tail(state[v, r]), picks[r]) for r in range(RC))

    one = jnp.where(lane == NV, 1.0, 0.0)
    picks = lax.fori_loop(0, NV, first, (one,) * RC)
    sums(picks, 0)

    count = (axes - 1) + jnp.where(rad < rads - 1, 1, 0) + jnp.where(row < rows - 1, axes, 0)
    for d in range(1, REACH + 1):
        count = count + jnp.where(rad >= d, 1, 0)
    pl.semaphore_wait(barrier, count)
    for d in range(2, REACH + 1):

        @pl.when(rad >= d)
        def _():
            pl.semaphore_signal(ready, inc=1, device_id={"rad": rad - d}, device_id_type=MESH)

    last = SWEEPS

    def of(p):
        return state if p == 0 else field.at[p - 1]

    def rad_copy(p, up):
        src = of(p)
        edge = RC - 1 if up else 0
        where = {"rad": rad + 1 if up else rad - 1}
        side = 0 if up else 1
        if p == last:
            return remote(src.at[PV, edge], radr.at[p, side, PV], s_rad.at[p, side], r_rad.at[p, side], where)
        return remote(src.at[:, edge], radr.at[p, side], s_rad.at[p, side], r_rad.at[p, side], where)

    def ax_copy(p, up):
        cell = 1 if up else 0
        where = {"ax": lax.rem(ax + (1 if up else axes - 1), axes)}
        side = 0 if up else 1
        if p == last:
            return remote(axs.at[p, cell, PV], axr.at[p, side, PV], s_ax.at[p, side], r_ax.at[p, side], where)
        return remote(axs.at[p, cell], axr.at[p, side], s_ax.at[p, side], r_ax.at[p, side], where)

    def total_copy(p, d):
        slot = 0 if d < REACH else 1
        return remote(t_src.at[p, slot], px.at[p, d - 1], s_px.at[p, d - 1], r_px.at[p, d - 1], {"rad": rad + d})

    def update(q, rm, rp, left, right, r, ghost, edge, keep):
        qm = jnp.where(lane == 0, ghost, pltpu.roll(q, 1, 1))
        b = q - qm
        f = jnp.where(lane == NX - 1, edge, pltpu.roll(b, NX - 1, 1))
        slope = jnp.maximum(jnp.minimum(b, f), 0.0) + jnp.minimum(jnp.maximum(b, f), 0.0)
        a = coef[0, r]
        g = a * q + coef[1, r] * slope
        flux_in = jnp.where(lane == 0, a * ghost, pltpu.roll(g, 1, 1))
        cm = jnp.where(sub == 0, left, pltpu.roll(q, 1, 0))
        cp = jnp.where(sub == CC - 1, right, pltpu.roll(q, CC - 1, 0))
        lap = (f - b) + (rm + rp) + (cm + cp) - 4.0 * q
        return q * keep + (flux_in - g) + coef[2, r] * lap

    def sweep(p, v, src, dst, pressures):
        keep = 1.0 - 0.5 * relax[v]
        fresh = []
        for r in range(RC):
            q = src[v, r]
            rm = radr[p, 0, v] if r == 0 else src[v, r - 1]
            rp = radr[p, 1, v] if r == RC - 1 else src[v, r + 1]
            left = axr[p, 0, v, r : r + 1, :]
            right = axr[p, 1, v, r : r + 1, :]
            ghost = pltpu.roll(ghosts[r], lax.rem(NX - v, NX), 1)
            edge = 0.0 if pressures is None else pressures[r] - q
            new = update(q, rm, rp, left, right, r, ghost, edge, keep)
            dst[v, r] = new
            fresh.append(new)
        return fresh

    swirl = None
    for p in range(SWEEPS + 1):
        src = of(p)
        for d in range(1, axes):
            remote(
                ms_src.at[p], ms_own.at[p, ax], s_own.at[p], r_own.at[p], {"ax": lax.rem(ax + d, axes)}
            ).start()
        if p >= 1:

            @pl.when(rad + 1 < rads)
            def _():
                total_copy(p, 1).start()

        @pl.when(rad < rads - 1)
        def _():
            rad_copy(p, True).start()

        @pl.when(rad > 0)
        def _():
            rad_copy(p, False).start()

        ax_copy(p, True).start()
        ax_copy(p, False).start()

        @pl.when(row < rows - 1)
        def _():
            for d in range(axes):
                remote(
                    ms_src.at[p], ms_up.at[p, ax], s_down.at[p], r_up.at[p], {"row": row + 1, "ax": d}
                ).start()

        if p == 1:

            @pl.when(rad + 2 < rads)
            def _():
                pl.semaphore_wait(ready, jnp.minimum(rads - 2 - rad, REACH - 1))

        if p >= 1:
            for d in range(2, REACH):

                @pl.when(rad + d < rads)
                def _():
                    total_copy(p, d).start()

        part = ms_own.at[p, pl.ds(0, axes - 1)]
        remote(part, part, s_own.at[p], r_own.at[p], {"ax": ax}).wait_recv()

        def mean(ref):
            total = ref[p, 0]
            for d in range(1, axes):
                total = total + ref[p, d]
            return total / jnp.broadcast_to(total[:, NV : NV + 1], (8, NX))

        profile = mean(ms_own)
        pressures = None
        if p >= 1:
            for d in range(1, REACH + 1):

                @pl.when(rad >= d)
                def _():
                    total_copy(p, d).wait_recv()

            before = px[p, 0]
            for d in range(2, REACH + 1):
                before = before + px[p, d - 1]
            if p < SWEEPS + 1:
                t_src[p, 1] = before + t_src[p, 0]

                @pl.when(rad + REACH < rads)
                def _():
                    total_copy(p, REACH).start()

            run = swirl
            for step in (1, 2, 4):
                run = run + jnp.where(sub >= step, pltpu.roll(run, step, 0), 0.0)
            scale = 4.0 / (RC * rads)
            pressure = jnp.broadcast_to(profile[:, PV : PV + 1], (8, NX)) + scale * ((run - swirl) + before)
            profile_s[...] = pressure
            rows_of = [profile_s[s : s + 1, :] for s in range(RC)]
            pressures = []
            for r in range(RC):
                st = hot[r]
                acc = jnp.broadcast_to(rows_of[0], (8, NX))
                for s in range(1, RC):
                    acc = jnp.where(st == float(s), rows_of[s], acc)
                pressures.append(acc)
        if p < SWEEPS:
            radius = 1.0 + (rad * RC + sub).astype(jnp.float32) / float(RC * rads)
            third = jnp.broadcast_to(profile[:, SV : SV + 1], (8, NX))
            swirl = third * third / radius
            t_src[p + 1, 0] = jnp.sum(swirl, axis=0, keepdims=True)

        @pl.when(row == 0)
        def _():
            upstream[...] = inlet_t[...]

        @pl.when(row > 0)
        def _():
            remote(ms_up.at[p], ms_up.at[p], s_down.at[p], r_up.at[p], {"ax": ax}).wait_recv()
            upstream[...] = mean(ms_up)

        for r in range(RC):
            st = hot[r]
            acc = jnp.broadcast_to(upstream[0:1, :], (8, NX))
            for s in range(1, RC):
                acc = jnp.where(st == float(s), upstream[s : s + 1, :], acc)
            ghosts[r] = acc

        @pl.when(rad > 0)
        def _():
            rad_copy(p, True).wait_recv()

        @pl.when(rad < rads - 1)
        def _():
            rad_copy(p, False).wait_recv()

        ax_copy(p, True).wait_recv()
        ax_copy(p, False).wait_recv()

        dst = field.at[p] if p + 1 < SWEEPS else out
        picks = (one,) * RC
        if p < SWEEPS:

            def plain(i, picks):
                v = i + jnp.where(i >= PV, 1, 0)
                fresh = sweep(p, v, src, dst, None)
                if p + 1 == SWEEPS:
                    return picks
                pack(dst, p + 1, v)
                return tuple(jnp.where(lane == v, tail(fresh[r]), picks[r]) for r in range(RC))

            picks = lax.fori_loop(0, NV - 1, plain, picks)
        if p == 0:
            for r in range(RC):
                field[0, PV, r] = state[PV, r]
        else:
            lagged = field.at[p] if p < SWEEPS else out
            fresh = sweep(p, PV, src, lagged, pressures)
        if p < SWEEPS:
            lagged = field.at[p]
            pack(lagged, p + 1, PV)
            picks = tuple(jnp.where(lane == PV, tail(lagged[PV, r]), picks[r]) for r in range(RC))
            sums(picks, p + 1)

        if p >= SWEEPS - 1:
            for v in range(NV):
                if (v == PV) == (p == SWEEPS):
                    wide = jnp.broadcast_to(profile[:, v : v + 1], (8, NX))
                    line = jnp.sum(jnp.where(diagonal, wide, 0.0), axis=0, keepdims=True)
                    out_profile[v : v + 1, :] = line[:, :RC]
            if p == SWEEPS:
                line = jnp.sum(jnp.where(diagonal, pressure, 0.0), axis=0, keepdims=True)
                out_pressure[...] = line[:, :RC]

    for p in range(SWEEPS + 1):
        part = ms_own.at[p, pl.ds(0, axes - 1)]
        remote(part, part, s_own.at[p], r_own.at[p], {"ax": ax}).wait_send()

        @pl.when(row < rows - 1)
        def _():
            remote(ms_up.at[p], ms_up.at[p], s_down.at[p], r_up.at[p], {"ax": ax}).wait_send()

        @pl.when(rad < rads - 1)
        def _():
            rad_copy(p, True).wait_send()

        @pl.when(rad > 0)
        def _():
            rad_copy(p, False).wait_send()

        ax_copy(p, True).wait_send()
        ax_copy(p, False).wait_send()
        if p >= 1:
            for d in range(1, REACH + 1):

                @pl.when(rad + d < rads)
                def _():
                    total_copy(p, d).wait_send()


def solution(mesh):
    sizes = (mesh.shape["row"], mesh.shape["rad"], mesh.shape["ax"])
    axes = sizes[2]
    phases = SWEEPS + 1

    def body(state, speed, visc, relax, area, station, flags, inlet):
        vmem = pl.BlockSpec(memory_space=pltpu.VMEM)
        smem = pl.BlockSpec(memory_space=pltpu.SMEM)
        f32 = jnp.float32
        dma = pltpu.SemaphoreType.DMA
        new, profile, pressure = pl.pallas_call(
            functools.partial(kernel, sizes),
            out_shape=(
                jax.ShapeDtypeStruct((NV, RC, CC, NX), f32),
                jax.ShapeDtypeStruct((NV, RC), f32),
                jax.ShapeDtypeStruct((1, RC), f32),
            ),
            in_specs=[vmem, vmem, vmem, smem, vmem, vmem, vmem, vmem],
            out_specs=(vmem, vmem, vmem),
            scratch_shapes=[
                pltpu.VMEM((SWEEPS, NV, RC, CC, NX), f32),
                pltpu.VMEM((phases, 2, NV, RC, NX), f32),
                pltpu.VMEM((phases, 2, NV, RC, NX), f32),
                pltpu.VMEM((phases, 2, NV, CC, NX), f32),
                pltpu.VMEM((phases, RC, NX), f32),
                pltpu.VMEM((phases, axes, RC, NX), f32),
                pltpu.VMEM((phases, axes, RC, NX), f32),
                pltpu.VMEM((phases, 2, 1, NX), f32),
                pltpu.VMEM((phases, REACH, 1, NX), f32),
                pltpu.VMEM((3, RC, CC, NX), f32),
                pltpu.VMEM((RC, RC, CC, NX), f32),
                pltpu.VMEM((RC, CC, NX), f32),
                pltpu.VMEM((RC, NX), f32),
                pltpu.VMEM((RC, NX), f32),
                pltpu.VMEM((RC, CC, NX), f32),
                pltpu.VMEM((RC, NX), f32),
                dma((phases, 2)),
                dma((phases, 2)),
                dma((phases, 2)),
                dma((phases, 2)),
                dma((phases,)),
                dma((phases,)),
                dma((phases,)),
                dma((phases,)),
                dma((phases, REACH)),
                dma((phases, REACH)),
                pltpu.SemaphoreType.REGULAR,
            ],
            compiler_params=pltpu.CompilerParams(
                collective_id=0, has_side_effects=True, vmem_limit_bytes=16 * 1024 * 1024
            ),
        )(
            state.reshape(NV, RC, CC, NX),
            speed.reshape(RC, CC, NX),
            visc.reshape(RC, CC, NX),
            relax,
            area.reshape(RC, CC),
            station.reshape(RC, CC),
            flags.reshape(RC, CC),
            inlet,
        )
        return new[:, None], profile[:, None], pressure

    return jax.shard_map(
        body,
        mesh=mesh,
        in_specs=(
            P(None, "row", "rad", "ax", None),
            P("row", "rad", "ax", None),
            P("row", "rad", "ax", None),
            P(),
            P("row", "rad", "ax"),
            P("row", "rad", "ax"),
            P("row", "rad", "ax"),
            P(None, "rad"),
        ),
        out_specs=(P(None, "row", "rad", "ax", None), P(None, "row", "rad"), P("row", "rad")),
        check_vma=False,
    )
```

time: 1070 us -> 53.2 us (0.05)
  the two profiles are of different devices: /device:TPU:409 before, /device:TPU:483 now
where the time goes in v1:
time: 53.2 us; the launch traced here: 52.9 us
  Pallas kernels  45.9 us (86%)
  local copies, waits for them, and re-layouts  6.29 us (12%)
  between operations  0.67 us (1%)
    pallas_call x1, Pallas kernels, body(): pl.pallas_call(functools.partial(kernel, sizes), out_shape=(jax.ShapeDtyp...  45.9 us
    unnamed x19, local copies, waits for them, and re-layouts  6.29 us

profile of v1, /device:TPU:483, one launch (start us, length us, event | category | flops | bytes accessed | tf_op | source)
XLA Modules:
  0.0 52.9 jit_solution(9642726407636386209)
XLA Ops:
  0.6 0.0 copy-start.4
  0.6 0.0 copy-start.3
  0.7 0.0 copy-start.7
  0.7 0.7 %copy-done.4 = s32[1,8,8]{2,1,0:T(8,128)S(1)} copy-done((s32[1,8,8]{2,1,0:T(8,128)S(1)}, s32[1,8,8]{2,1,0:T(8,128)}, u32[]{:S(2)}) %copy-start.4) | copy-done | bytes 280
  1.3 0.0 copy-done.3
  1.3 0.0 copy-done.7
  1.3 0.0 copy-start
  1.3 0.9 %copy-done = f32[7,1,8,8,128]{4,3,2,1,0:T(8,128)S(1)} copy-done((f32[7,1,8,8,128]{4,3,2,1,0:T(8,128)S(1)}, f32[7,1,8,8,128]{4,3,2,1,0:T(8,128)}, u32[]{:S(2)}) %copy-start) | copy-done | bytes 229400
  2.3 0.0 copy-start.1
  2.3 0.8 %copy-done.1 = f32[1,8,8,128]{3,2,1,0:T(8,128)S(1)} copy-done((f32[1,8,8,128]{3,2,1,0:T(8,128)S(1)}, f32[1,8,8,128]{3,2,1,0:T(8,128)}, u32[]{:S(2)}) %copy-start.1) | copy-done | bytes 32792
  3.0 0.0 copy-start.2
  3.0 0.8 %copy-done.2 = f32[1,8,8,128]{3,2,1,0:T(8,128)S(1)} copy-done((f32[1,8,8,128]{3,2,1,0:T(8,128)S(1)}, f32[1,8,8,128]{3,2,1,0:T(8,128)}, u32[]{:S(2)}) %copy-start.2) | copy-done | bytes 32792
  3.8 0.0 copy-start.5
  3.8 0.7 %copy-done.5 = s32[1,8,8]{2,1,0:T(8,128)S(1)} copy-done((s32[1,8,8]{2,1,0:T(8,128)S(1)}, s32[1,8,8]{2,1,0:T(8,128)}, u32[]{:S(2)}) %copy-start.5) | copy-done | bytes 280
  4.5 0.0 copy-start.6
  4.5 0.7 %copy-done.6 = f32[7,8]{1,0:T(8,128)S(1)} copy-done((f32[7,8]{1,0:T(8,128)S(1)}, f32[7,8]{1,0:T(8,128)}, u32[]{:S(2)}) %copy-start.6) | copy-done | bytes 248
  5.2 45.9 %shard_map.103 = (f32[7,8,8,128]{3,2,1,0:T(8,128)S(1)}, f32[7,8]{1,0:T(8,128)S(1)}, f32[1,8]{1,0:T(1,128)S(1)}) custom-call(f32[7,8,8,128]{3,2,1,0:T(8,128)S(1)} %bitcast.11, f32[8,8,128]{2,1,0:T(8,128)S(1)} %bitcast.12, f32[8,8,128]{2,1,0:T(8,128)S(1)} %bitcast.13, f32[7]{0:T(128)S(1)} %copy-done.7, f32[8,8]{1,0:T(8,128)S(1)} %bitcast.14, ...), custom_call_target="tpu_custom_call" | custom-call | tf_op jit(solution)/shard_map/pallas_call | solution.py:416
  51.1 0.6 %copy.12 = f32[7,1,8]{2,1,0:T(1,128)} copy(f32[7,1,8]{2,0,1:T(8,128)S(1)} %bitcast.17) | data formatting | bytes 448
  51.7 0.7 %copy.15 = f32[7,1,8,8,128]{4,3,2,1,0:T(8,128)} copy(f32[7,1,8,8,128]{4,3,2,1,0:T(8,128)S(1)} %bitcast.10) | data formatting | bytes 458752
  52.4 0.5 copy.16
Async XLA Ops:
  0.6 0.7 %copy-start.4 = (s32[1,8,8]{2,1,0:T(8,128)S(1)}, s32[1,8,8]{2,1,0:T(8,128)}, u32[]{:S(2)}) copy-start(s32[1,8,8]{2,1,0:T(8,128)} %param.13) | copy-start | bytes 772
  0.6 0.7 %copy-start.3 = (f32[1,8,8]{2,1,0:T(8,128)S(1)}, f32[1,8,8]{2,1,0:T(8,128)}, u32[]{:S(2)}) copy-start(f32[1,8,8]{2,1,0:T(8,128)} %param.12) | copy-start | bytes 772
  0.7 0.7 %copy-start.7 = (f32[7]{0:T(128)S(1)}, f32[7]{0:T(128)}, u32[]{:S(2)}) copy-start(f32[7]{0:T(128)} %relax.1) | copy-start | bytes 88
  1.3 0.9 %copy-start = (f32[7,1,8,8,128]{4,3,2,1,0:T(8,128)S(1)}, f32[7,1,8,8,128]{4,3,2,1,0:T(8,128)}, u32[]{:S(2)}) copy-start(f32[7,1,8,8,128]{4,3,2,1,0:T(8,128)} %param.8) | copy-start | bytes 688132
  2.3 0.8 %copy-start.1 = (f32[1,8,8,128]{3,2,1,0:T(8,128)S(1)}, f32[1,8,8,128]{3,2,1,0:T(8,128)}, u32[]{:S(2)}) copy-start(f32[1,8,8,128]{3,2,1,0:T(8,128)} %param.9) | copy-start | bytes 98308
  3.0 0.8 %copy-start.2 = (f32[1,8,8,128]{3,2,1,0:T(8,128)S(1)}, f32[1,8,8,128]{3,2,1,0:T(8,128)}, u32[]{:S(2)}) copy-start(f32[1,8,8,128]{3,2,1,0:T(8,128)} %param.10) | copy-start | bytes 98308
  3.8 0.7 %copy-start.5 = (s32[1,8,8]{2,1,0:T(8,128)S(1)}, s32[1,8,8]{2,1,0:T(8,128)}, u32[]{:S(2)}) copy-start(s32[1,8,8]{2,1,0:T(8,128)} %param.14) | copy-start | bytes 772
  4.5 0.7 %copy-start.6 = (f32[7,8]{1,0:T(8,128)S(1)}, f32[7,8]{1,0:T(8,128)}, u32[]{:S(2)}) copy-start(f32[7,8]{1,0:T(8,128)} %inlet.1) | copy-start | bytes 676

commit v2 on v1

v2 whole, which is shorter than its diff:
```python
import functools

import jax
import jax.numpy as jnp
from jax import lax
from jax.experimental import pallas as pl
from jax.experimental.pallas import tpu as pltpu
from jax.sharding import PartitionSpec as P

MESH = pl.DeviceIdType.MESH
SWEEPS = 4
NV = 7
PV = 4
SV = 3
RC = 8
CC = 8
NX = 128
BASE = (-1, -1, -1, -1, 2, 2, 2, 5, 4, 6, 6, 7, 7, 10, 9, 8)
DIRECT = 6
TX = 8


def kernel(
    sizes,
    state_h,
    speed_h,
    visc_h,
    relax_h,
    area_h,
    station_h,
    flags_h,
    inlet_h,
    out,
    out_profile,
    out_pressure,
    field,
    axs,
    axr,
    radr,
    ms_src,
    ms_own,
    ms_up,
    t_src,
    px,
    coef,
    weight,
    hot,
    upstream,
    inlet_t,
    ghosts,
    profile_s,
    tm_src,
    tm_own,
    tr,
    s_ax,
    r_ax,
    s_rad,
    r_rad,
    s_own,
    r_own,
    s_down,
    r_up,
    s_px,
    r_px,
    s_tm,
    r_tm,
    s_tr,
    r_tr,
    ready,
    state,
    speed,
    visc,
    relax,
    area,
    station,
    flags,
    inlet,
    s_in,
):
    rows, rads, axes = sizes
    row, rad, ax = lax.axis_index("row"), lax.axis_index("rad"), lax.axis_index("ax")
    lane = lax.broadcasted_iota(jnp.int32, (8, NX), 1)
    sub = lax.broadcasted_iota(jnp.int32, (8, NX), 0)
    zero = jnp.zeros((8, NX), jnp.float32)

    def remote(src, dst, ssem, rsem, where):
        return pltpu.make_async_remote_copy(
            src_ref=src, dst_ref=dst, send_sem=ssem, recv_sem=rsem, device_id=where, device_id_type=MESH
        )

    barrier = pltpu.get_barrier_semaphore()

    def greet(where):
        pl.semaphore_signal(barrier, inc=1, device_id=where, device_id_type=MESH)

    for d in range(1, axes):
        greet({"ax": lax.rem(ax + d, axes)})

    heard = [[r for r in range(BASE[x] + 1, x)] for x in range(rads)]
    own_pairs = [(r, x) for x in range(rads) for r in heard[x] if r < x - 1]
    sum_pairs = [(BASE[x], x) for x in range(rads) if BASE[x] >= 0]

    def table(values):
        out = jnp.int32(0)
        for i, value in enumerate(values):
            if value:
                out = out + jnp.where(rad == i, value, 0)
        return out

    def among(which):
        mask = sum(1 << r for r in which)
        return (lax.shift_right_logical(jnp.int32(mask), rad) & 1) == 1

    def distances(pairs):
        return [(d, [r for r, x in pairs if x - r == d]) for d in sorted({x - r for r, x in pairs})]

    @pl.when(rad > 0)
    def _():
        greet({"rad": rad - 1})

    @pl.when(rad < rads - 1)
    def _():
        greet({"rad": rad + 1})

    for d, senders in distances(own_pairs + sum_pairs):

        @pl.when(among(senders))
        def _():
            greet({"rad": rad + d})

    @pl.when(row > 0)
    def _():
        for d in range(axes):
            greet({"row": row - 1, "ax": d})

    first_part, second_part = [
        [pltpu.make_async_copy(src, dst, s_in.at[k, i]) for i, (src, dst) in enumerate(pairs)]
        for k, pairs in enumerate(
            (
                (
                    (area_h, area),
                    (station_h, station),
                    (state_h.at[pl.ds(SV, 2)], state.at[pl.ds(SV, 2)]),
                ),
                (
                    (flags_h, flags),
                    (speed_h, speed),
                    (visc_h, visc),
                    (relax_h, relax),
                    (inlet_h, inlet),
                    (state_h.at[pl.ds(0, SV)], state.at[pl.ds(0, SV)]),
                    (state_h.at[pl.ds(PV + 1, NV - PV - 1)], state.at[pl.ds(PV + 1, NV - PV - 1)]),
                ),
            )
        )
    ]
    for load in first_part + second_part:
        load.start()

    @pl.when(rad == 0)
    def _():
        radr[:, 0] = jnp.zeros_like(radr[:, 0])
        tr[:, 0] = jnp.zeros_like(tr[:, 0])

    @pl.when(rad == rads - 1)
    def _():
        radr[:, 1] = jnp.zeros_like(radr[:, 1])
        tr[:, 1] = jnp.zeros_like(tr[:, 1])

    for d in range(1, DIRECT + 1):

        @pl.when(jnp.logical_not(among([x for x in range(rads) if x - d in heard[x]])))
        def _():
            px[:, d - 1] = jnp.zeros_like(px[:, d - 1])

    @pl.when(among([x for x in range(rads) if BASE[x] < 0]))
    def _():
        px[:, DIRECT] = jnp.zeros_like(px[:, DIRECT])

    diagonal = sub == lane

    def column(ref, r):
        wide = jnp.broadcast_to(ref[r : r + 1, :], (8, 8))
        return jnp.broadcast_to(jnp.sum(jnp.where(diagonal[:, :8], wide, 0.0), axis=1, keepdims=True), (8, NX))

    def greeted():
        fixed = [0] * rads
        for _, x in own_pairs + sum_pairs:
            fixed[x] += 1
        for x in range(rads):
            fixed[x] += (x > 0) + (x < rads - 1)
        pl.semaphore_wait(barrier, (axes - 1) + table(fixed) + jnp.where(row < rows - 1, axes, 0))
        for which, pairs in enumerate((own_pairs, sum_pairs)):
            for d, senders in distances(pairs):

                @pl.when(among([r + d for r in senders]))
                def _():
                    pl.semaphore_signal(ready.at[which], inc=1, device_id={"rad": rad - d}, device_id_type=MESH)

    def await_ready(which):
        counts = [0] * rads
        for r, _ in (own_pairs, sum_pairs)[which]:
            counts[r] += 1

        @pl.when(among([r for r in range(rads) if counts[r]]))
        def _():
            pl.semaphore_wait(ready.at[which], table(counts))

    last = SWEEPS

    group = lax.rem(lane, 64) // TX
    half = lane // 64
    spot = lax.rem(lane, TX)

    def tail_pack(rows_of, both):
        acc = zero
        for r in range(RC):
            for h in range(1 if both else 2):
                moved = pltpu.roll(rows_of(h, r), (TX * (r + 1) + 64 * h) % NX, 1)
                acc = jnp.where((group == r) & (half == h), moved, acc)
        if both:
            acc = jnp.where(half == 0, acc, pltpu.roll(acc, 64, 1))
        return acc

    def tail_copy(p, d):
        n = 2 * RC if p < last else RC
        return remote(
            tm_src.at[p, pl.ds(0, n)],
            tm_own.at[p, ax, pl.ds(0, n)],
            s_tm.at[p],
            r_tm.at[p],
            {"ax": lax.rem(ax + d, axes)},
        )

    def tail_all(p):
        n = 2 * RC if p < last else RC
        part = tm_own.at[p, pl.ds(0, axes - 1), pl.ds(0, n)]
        return remote(part, part, s_tm.at[p], r_tm.at[p], {"ax": ax})

    def tail_rad(p, up):
        side = 0 if up else 1
        where = {"rad": rad + 1 if up else rad - 1}
        return remote(
            tm_src.at[p, pl.ds(RC, RC)], tr.at[p, side], s_tr.at[p, side], r_tr.at[p, side], where
        )

    def total_copy(k, d):
        return remote(t_src.at[k, 0], px.at[k, d - 1], s_px.at[k, d - 1], r_px.at[k, d - 1], {"rad": rad + d})

    def sum_copy(k, d):
        where = {"rad": rad + d}
        return remote(t_src.at[k, 1], px.at[k, DIRECT], s_px.at[k, DIRECT + d - 1], r_px.at[k, DIRECT], where)

    own_steps = distances(own_pairs + [(x - 1, x) for x in range(1, rads)])
    sum_steps = distances(sum_pairs)

    for load in first_part:
        load.wait()
    areas = area[...]
    local_station = (station[...] - rad * RC).astype(jnp.float32)
    tail_station = zero
    tail_area = zero
    for r in range(RC):
        st = column(local_station, r)
        ar = column(areas, r)
        hot[r] = st
        for s in range(RC):
            weight[s, r] = jnp.where(st == float(s), ar, 0.0)
        mine = group == r
        tail_station = jnp.where(mine, st, tail_station)
        tail_area = jnp.where(mine & ((spot == TX - 1) | ((spot == TX - 2) & (half == 0))), ar, tail_area)
    counted = (spot == TX - 2) & (half == 0)

    def tail_send(p, q):
        q = jnp.where(counted, 1.0, q)
        total = zero
        for s in range(RC):
            part = jnp.sum(jnp.where(tail_station == float(s), tail_area, 0.0) * q, axis=0, keepdims=True)
            total = jnp.where(sub == s, part, total)
        tm_src[p, 0:RC] = total
        tm_own[p, ax, 0:RC] = total
        for d in range(1, axes):
            tail_copy(p, d).start()
        if p < last:

            @pl.when(rad > 0)
            def _():
                tail_rad(p, False).start()

            @pl.when(rad < rads - 1)
            def _():
                tail_rad(p, True).start()

        if p == last:

            @pl.when(row < rows - 1)
            def _():
                for d in range(axes):
                    up_copy(p, d).start()

    def up_copy(p, d):
        src = tm_src.at[p, pl.ds(0, RC)] if p == last else ms_src.at[p]
        return remote(src, ms_up.at[p, ax], s_down.at[p], r_up.at[p], {"row": row + 1, "ax": d})

    def fold(total):
        for step in (8, 16, 32):
            total = total + pltpu.roll(total, step, 1)
        return total

    def at(x, i):
        return jnp.broadcast_to(x[:, i : i + 1], (8, NX))

    tail = tail_pack(lambda h, r: state[SV + h, r], False)
    tm_src[0, RC:] = tail
    greeted()
    tail_send(0, tail)

    def sums(picks, p):
        total = zero
        for s in range(RC):
            acc = weight[s, 0] * picks[0]
            for r in range(1, RC):
                acc = acc + weight[s, r] * picks[r]
            total = jnp.where(sub == s, jnp.sum(acc, axis=0, keepdims=True), total)
        ms_src[p] = total
        if p == last - 1:
            ms_own[ax] = total

    def pack(src, p, v):
        for r in range(RC):
            axs[p, 0, v, r : r + 1, :] = src[v, r, 0:1, :]
            axs[p, 1, v, r : r + 1, :] = src[v, r, CC - 1 : CC, :]

    def of(p):
        return state if p == 0 else field.at[p - 1]

    def rad_copy(p, up):
        src = of(p)
        edge = RC - 1 if up else 0
        where = {"rad": rad + 1 if up else rad - 1}
        side = 0 if up else 1
        if p == last:
            return remote(src.at[PV, edge], radr.at[p, side, PV], s_rad.at[p, side], r_rad.at[p, side], where)
        return remote(src.at[:, edge], radr.at[p, side], s_rad.at[p, side], r_rad.at[p, side], where)

    def ax_copy(p, up):
        cell = 1 if up else 0
        where = {"ax": lax.rem(ax + (1 if up else axes - 1), axes)}
        side = 0 if up else 1
        if p == last:
            return remote(axs.at[p, cell, PV], axr.at[p, side, PV], s_ax.at[p, side], r_ax.at[p, side], where)
        return remote(axs.at[p, cell], axr.at[p, side], s_ax.at[p, side], r_ax.at[p, side], where)

    def own_copy(d):
        return remote(ms_src.at[last - 1], ms_own.at[ax], s_own, r_own, {"ax": lax.rem(ax + d, axes)})

    def field_send(p):
        if p < last:

            @pl.when(row < rows - 1)
            def _():
                for d in range(axes):
                    up_copy(p, d).start()

        @pl.when(rad < rads - 1)
        def _():
            rad_copy(p, True).start()

        @pl.when(rad > 0)
        def _():
            rad_copy(p, False).start()

        ax_copy(p, True).start()
        ax_copy(p, False).start()
        if p == last - 1:
            for d in range(1, axes):
                own_copy(d).start()

    def update(q, rm, rp, left, right, coefs, ghost, edge, keep):
        a, ah, nu = coefs
        qm = jnp.where(lane == 0, ghost, pltpu.roll(q, 1, 1))
        b = q - qm
        f = jnp.where(lane == NX - 1, edge, pltpu.roll(b, NX - 1, 1))
        slope = jnp.maximum(jnp.minimum(b, f), 0.0) + jnp.minimum(jnp.maximum(b, f), 0.0)
        g = a * q + ah * slope
        flux_in = jnp.where(lane == 0, a * ghost, pltpu.roll(g, 1, 1))
        cm = jnp.where(sub == 0, left, pltpu.roll(q, 1, 0))
        cp = jnp.where(sub == CC - 1, right, pltpu.roll(q, CC - 1, 0))
        lap = (f - b) + (rm + rp) + (cm + cp) - 4.0 * q
        return q * keep + (flux_in - g) + nu * lap

    def tail_update(p, q, ghost):
        left = tm_own[p, lax.rem(ax + axes - 1, axes), 2 * RC - 1 : 2 * RC]
        right = tm_own[p, lax.rem(ax + 1, axes), RC : RC + 1]
        a, ah, nu, keep = tail_coefs
        b = q - pltpu.roll(q, 1, 1)
        edge = 0.0 if ghost is None else jnp.where(half == 0, 0.0, ghost - q)
        f = jnp.where(spot == TX - 1, edge, pltpu.roll(b, NX - 1, 1))
        slope = jnp.maximum(jnp.minimum(b, f), 0.0) + jnp.minimum(jnp.maximum(b, f), 0.0)
        g = a * q + ah * slope
        rm = jnp.where(group == 0, pltpu.roll(tr[p, 0], 72, 1), pltpu.roll(q, TX, 1))
        rp = jnp.where(group == RC - 1, pltpu.roll(tr[p, 1], 56, 1), pltpu.roll(q, NX - TX, 1))
        cm = jnp.where(sub == 0, left, pltpu.roll(q, 1, 0))
        cp = jnp.where(sub == CC - 1, right, pltpu.roll(q, CC - 1, 0))
        lap = (f - b) + (rm + rp) + (cm + cp) - 4.0 * q
        new = q * keep + (pltpu.roll(g, 1, 1) - g) + nu * lap
        return jnp.where(half == 0, new, q) if ghost is None else new

    def sweep(p, v, src, dst, pressures):
        keep = 1.0 - 0.5 * relax[v]
        fresh = []
        for r in range(RC):
            q = src[v, r]
            rm = radr[p, 0, v] if r == 0 else src[v, r - 1]
            rp = radr[p, 1, v] if r == RC - 1 else src[v, r + 1]
            left = axr[p, 0, v, r : r + 1, :]
            right = axr[p, 1, v, r : r + 1, :]
            ghost = pltpu.roll(ghosts[r], (NX - v) % NX if isinstance(v, int) else lax.rem(NX - v, NX), 1)
            edge = 0.0 if pressures is None else pressures[r] - q
            new = update(q, rm, rp, left, right, (coef[0, r], coef[1, r], coef[2, r]), ghost, edge, keep)
            dst[v, r] = new
            fresh.append(new)
        return fresh

    for load in second_part:
        load.wait()
    one = jnp.where(lane == NV, 1.0, 0.0)

    def first(v, picks):
        pack(state, 0, v)
        return tuple(jnp.where(lane == v, at(state[v, r], NX - 1), picks[r]) for r in range(RC))

    sums(lax.fori_loop(0, NV, first, (one,) * RC), 0)
    field_send(0)

    flag = flags[...].astype(jnp.float32)
    tail_flag = zero
    for r in range(RC):
        fl = 0.5 * column(flag, r)
        tail_flag = jnp.where(group == r, fl, tail_flag)
        a = 0.5 * speed[r]
        coef[0, r] = a
        coef[1, r] = a * fl
        coef[2, r] = 0.5 * visc[r]
        field[0, PV, r] = state[PV, r]
    tail_a = tail_pack(lambda h, r: coef[0, r], True)
    tail_coefs = (
        tail_a,
        tail_a * tail_flag,
        tail_pack(lambda h, r: coef[2, r], True),
        1.0 - 0.5 * jnp.where(half == 0, relax[SV], relax[PV]),
    )
    turned = zero
    inlet_all = inlet[...]
    for v in range(NV):
        turned = jnp.where(lane == v, column(inlet_all, v), turned)
    inlet_t[...] = turned
    radius = 1.0 + (rad * RC + sub).astype(jnp.float32) / float(RC * rads)

    def write_profile(v, wide):
        line = jnp.sum(jnp.where(diagonal, wide, 0.0), axis=0, keepdims=True)
        out_profile[v : v + 1, :] = line[:, :RC]

    def total_of(load):
        total = load(0)
        for d in range(1, axes):
            total = total + load(d)
        return total

    swirl = None
    for p in range(SWEEPS + 1):
        tail_all(p).wait_recv()
        if p < last:

            @pl.when(rad > 0)
            def _():
                tail_rad(p, True).wait_recv()

            @pl.when(rad < rads - 1)
            def _():
                tail_rad(p, False).wait_recv()

        folded = fold(total_of(lambda d: tm_own[p, d, 0:RC]))
        areas_in = at(folded, 62)
        ghost = None
        if p >= 1:
            for d, senders in own_steps:

                @pl.when(among([r + d for r in senders]))
                def _():
                    total_copy(p - 1, d).wait_recv()

            @pl.when(among([x for x in range(rads) if BASE[x] >= 0]))
            def _():
                sum_copy(p - 1, 1).wait_recv()

            before = jnp.sum(px[p - 1], axis=0)
            t_src[p - 1, 1] = before + t_src[p - 1, 0]
            if p == 1:
                await_ready(1)
            for d, senders in sum_steps:

                @pl.when(among(senders))
                def _():
                    sum_copy(p - 1, d).start()

            run = swirl
            for step in (1, 2, 4):
                run = run + jnp.where(sub >= step, pltpu.roll(run, step, 0), 0.0)
            scale = 4.0 / (RC * rads)
            fourth = at(folded, 127) / areas_in
            pressure = fourth + scale * ((run - swirl) + before)
            profile_s[...] = pressure
            rows_of = [profile_s[s : s + 1, :] for s in range(RC)]
            if p < last:
                ghost = jnp.broadcast_to(rows_of[0], (8, NX))
                for s in range(1, RC):
                    ghost = jnp.where(tail_station == float(s), rows_of[s], ghost)
        if p < last:
            third = at(folded, 63) / areas_in
            swirl = third * third / radius
            t_src[p, 0] = jnp.sum(swirl, axis=0, keepdims=True)
            tail = tail_update(p, tail, ghost)
            if p + 1 < last:
                tm_src[p + 1, RC:] = tail
            tail_send(p + 1, tail)

            if p == 0:
                await_ready(0)
            for d, senders in own_steps:

                @pl.when(among(senders))
                def _():
                    total_copy(p, d).start()

        src = of(p)

        @pl.when(row == 0)
        def _():
            upstream[...] = inlet_t[...]

        @pl.when(row > 0)
        def _():
            remote(ms_up.at[p], ms_up.at[p], s_down.at[p], r_up.at[p], {"ax": ax}).wait_recv()
            total = total_of(lambda d: ms_up[p, d])
            if p == last:
                total = fold(total)
                upstream[...] = at(total, 127) / at(total, 62)
            else:
                upstream[...] = total / at(total, NV)

        for r in range(RC):
            st = hot[r]
            acc = jnp.broadcast_to(upstream[0:1, :], (8, NX))
            for s in range(1, RC):
                acc = jnp.where(st == float(s), upstream[s : s + 1, :], acc)
            ghosts[r] = acc

        @pl.when(rad > 0)
        def _():
            rad_copy(p, True).wait_recv()

        @pl.when(rad < rads - 1)
        def _():
            rad_copy(p, False).wait_recv()

        ax_copy(p, True).wait_recv()
        ax_copy(p, False).wait_recv()

        dst = field.at[p] if p + 1 < SWEEPS else out
        picks = (one,) * RC
        if p < SWEEPS:

            def plain(i, picks):
                v = i + (1 if i >= PV else 0)
                fresh = sweep(p, v, src, dst, None)
                if p + 1 == SWEEPS:
                    return picks
                pack(dst, p + 1, v)
                return tuple(jnp.where(lane == v, at(fresh[r], NX - 1), picks[r]) for r in range(RC))

            for i in range(NV - 1):
                picks = plain(i, picks)
        if p > 0:
            pressures = []
            for r in range(RC):
                st = hot[r]
                acc = jnp.broadcast_to(rows_of[0], (8, NX))
                for s in range(1, RC):
                    acc = jnp.where(st == float(s), rows_of[s], acc)
                pressures.append(acc)
            fresh = sweep(p, PV, src, field.at[p] if p < SWEEPS else out, pressures)
        else:
            fresh = [state[PV, r] for r in range(RC)]
        if p < SWEEPS:
            pack(field.at[p], p + 1, PV)
            if p + 1 < SWEEPS:
                sums(tuple(jnp.where(lane == PV, at(fresh[r], NX - 1), picks[r]) for r in range(RC)), p + 1)
            field_send(p + 1)

    remote(ms_own.at[pl.ds(0, axes - 1)], ms_own.at[pl.ds(0, axes - 1)], s_own, r_own, {"ax": ax}).wait_recv()
    total = total_of(lambda d: ms_own[d])
    profile = total / at(total, NV)
    for v in range(NV):
        write_profile(v, fourth if v == PV else at(profile, v))
    out_pressure[...] = jnp.sum(jnp.where(diagonal, pressure, 0.0), axis=0, keepdims=True)[:, :RC]

    remote(ms_own.at[pl.ds(0, axes - 1)], ms_own.at[pl.ds(0, axes - 1)], s_own, r_own, {"ax": ax}).wait_send()
    for p in range(SWEEPS + 1):
        tail_all(p).wait_send()

        @pl.when(row < rows - 1)
        def _():
            remote(ms_up.at[p], ms_up.at[p], s_down.at[p], r_up.at[p], {"ax": ax}).wait_send()

        @pl.when(rad < rads - 1)
        def _():
            rad_copy(p, True).wait_send()
            if p < last:
                tail_rad(p, True).wait_send()

        @pl.when(rad > 0)
        def _():
            rad_copy(p, False).wait_send()
            if p < last:
                tail_rad(p, False).wait_send()

        ax_copy(p, True).wait_send()
        ax_copy(p, False).wait_send()
        if p < last:
            for d, senders in own_steps:

                @pl.when(among(senders))
                def _():
                    total_copy(p, d).wait_send()

            for d, senders in sum_steps:

                @pl.when(among(senders))
                def _():
                    sum_copy(p, d).wait_send()


def solution(mesh):
    sizes = (mesh.shape["row"], mesh.shape["rad"], mesh.shape["ax"])
    axes = sizes[2]
    phases = SWEEPS + 1

    def body(state, speed, visc, relax, area, station, flags, inlet):
        vmem = pl.BlockSpec(memory_space=pltpu.VMEM)
        hbm = pl.BlockSpec(memory_space=pltpu.HBM)
        f32 = jnp.float32
        dma = pltpu.SemaphoreType.DMA
        new, profile, pressure = pl.pallas_call(
            functools.partial(kernel, sizes),
            out_shape=(
                jax.ShapeDtypeStruct((NV, RC, CC, NX), f32),
                jax.ShapeDtypeStruct((NV, RC), f32),
                jax.ShapeDtypeStruct((1, RC), f32),
            ),
            in_specs=[hbm] * 8,
            out_specs=(vmem, vmem, vmem),
            scratch_shapes=[
                pltpu.VMEM((SWEEPS, NV, RC, CC, NX), f32),
                pltpu.VMEM((phases, 2, NV, RC, NX), f32),
                pltpu.VMEM((phases, 2, NV, RC, NX), f32),
                pltpu.VMEM((phases, 2, NV, CC, NX), f32),
                pltpu.VMEM((phases, RC, NX), f32),
                pltpu.VMEM((axes, RC, NX), f32),
                pltpu.VMEM((phases, axes, RC, NX), f32),
                pltpu.VMEM((SWEEPS, 2, 1, NX), f32),
                pltpu.VMEM((SWEEPS, DIRECT + 1, 1, NX), f32),
                pltpu.VMEM((3, RC, CC, NX), f32),
                pltpu.VMEM((RC, RC, CC, NX), f32),
                pltpu.VMEM((RC, CC, NX), f32),
                pltpu.VMEM((RC, NX), f32),
                pltpu.VMEM((RC, NX), f32),
                pltpu.VMEM((RC, CC, NX), f32),
                pltpu.VMEM((RC, NX), f32),
                pltpu.VMEM((phases, 2 * RC, NX), f32),
                pltpu.VMEM((phases, axes, 2 * RC, NX), f32),
                pltpu.VMEM((SWEEPS, 2, CC, NX), f32),
                dma((phases, 2)),
                dma((phases, 2)),
                dma((phases, 2)),
                dma((phases, 2)),
                dma,
                dma,
                dma((phases,)),
                dma((phases,)),
                dma((SWEEPS, 2 * DIRECT + 1)),
                dma((SWEEPS, DIRECT + 1)),
                dma((phases,)),
                dma((phases,)),
                dma((SWEEPS, 2)),
                dma((SWEEPS, 2)),
                pltpu.SemaphoreType.REGULAR((2,)),
                pltpu.VMEM((NV, RC, CC, NX), f32),
                pltpu.VMEM((RC, CC, NX), f32),
                pltpu.VMEM((RC, CC, NX), f32),
                pltpu.SMEM((NV,), f32),
                pltpu.VMEM((RC, CC), f32),
                pltpu.VMEM((RC, CC), jnp.int32),
                pltpu.VMEM((RC, CC), jnp.int32),
                pltpu.VMEM((NV, RC), f32),
                dma((2, 8)),
            ],
            compiler_params=pltpu.CompilerParams(
                collective_id=0, has_side_effects=True, vmem_limit_bytes=16 * 1024 * 1024
            ),
        )(
            *[
                pltpu.with_memory_space_constraint(x, pltpu.HBM)
                for x in (
                    state.reshape(NV, RC, CC, NX),
                    speed.reshape(RC, CC, NX),
                    visc.reshape(RC, CC, NX),
                    relax,
                    area.reshape(RC, CC),
                    station.reshape(RC, CC),
                    flags.reshape(RC, CC),
                    inlet,
                )
            ]
        )
        return new[:, None], profile[:, None], pressure

    return jax.shard_map(
        body,
        mesh=mesh,
        in_specs=(
            P(None, "row", "rad", "ax", None),
            P("row", "rad", "ax", None),
            P("row", "rad", "ax", None),
            P(),
            P("row", "rad", "ax"),
            P("row", "rad", "ax"),
            P("row", "rad", "ax"),
            P(None, "rad"),
        ),
        out_specs=(P(None, "row", "rad", "ax", None), P(None, "row", "rad"), P("row", "rad")),
        check_vma=False,
    )
```

time: 53.2 us -> 41.1 us (0.77)
  Pallas kernels: 45.9 us -> 38.6 us
  local copies, waits for them, and re-layouts: 6.29 us -> 1.78 us
    pallas_call x1, Pallas kernels: 45.9 us -> 38.6 us  [body(): pl.pallas_call(functools.partial(kernel, sizes), out_shape=(jax.ShapeDtyp...]
    unnamed x19 -> x3, local copies, waits for them, and re-layouts: 6.29 us -> 1.78 us
where the time goes in v2:
time: 41.1 us; the launch traced here: 41 us
  Pallas kernels  38.6 us (94%)
  local copies, waits for them, and re-layouts  1.78 us (4%)
  between operations  0.64 us (2%)
    pallas_call x1, Pallas kernels, body(): pl.pallas_call(functools.partial(kernel, sizes), out_shape=(jax.ShapeDtyp...  38.6 us
    unnamed x3, local copies, waits for them, and re-layouts  1.78 us

profile of v2, /device:TPU:483, one launch (start us, length us, event | category | flops | bytes accessed | tf_op | source)
XLA Modules:
  0.0 41.0 jit_solution(8599431317020264710)
XLA Ops:
  0.6 38.6 %shard_map.103 = (f32[7,8,8,128]{3,2,1,0:T(8,128)S(1)}, f32[7,8]{1,0:T(8,128)S(1)}, f32[1,8]{1,0:T(1,128)S(1)}) custom-call(f32[7,8,8,128]{3,2,1,0:T(8,128)} %bitcast.12, f32[8,8,128]{2,1,0:T(8,128)} %bitcast.13, f32[8,8,128]{2,1,0:T(8,128)} %bitcast.14, f32[7]{0:T(128)} %relax_h.1, f32[8,8]{1,0:T(8,128)} %bitcast.15, s32[8,8]{1,0:T(8,128)} %bitcast.16, ...), custom_call_target="tpu_custom_call" | custom-call | tf_op jit(solution)/shard_map/pallas_call | solution.py:654
  39.2 0.6 %copy.12 = f32[7,1,8]{2,1,0:T(1,128)} copy(f32[7,1,8]{2,0,1:T(8,128)S(1)} %bitcast.11) | data formatting | bytes 448
  39.8 0.7 %copy.15 = f32[7,1,8,8,128]{4,3,2,1,0:T(8,128)} copy(f32[7,1,8,8,128]{4,3,2,1,0:T(8,128)S(1)} %bitcast.10) | data formatting | bytes 458752
  40.5 0.5 %copy.16 = f32[1,8]{1,0:T(1,128)} copy(f32[1,8]{1,0:T(1,128)S(1)} %get-tuple-element.17) | data formatting | bytes 64

commit v3 on v2

--- a/solution.py
+++ b/solution.py
@@ -15,7 +15,7 @@
 RC = 8
 CC = 8
 NX = 128
-BASE = (-1, -1, -1, -1, 2, 2, 2, 5, 4, 6, 6, 7, 7, 10, 9, 8)
+BASE = (-1, -1, -1, -1, 1, 3, 2, 4, 4, 6, 6, 6, 7, 8, 10, 9)
 DIRECT = 6
 TX = 8
 
@@ -52,6 +52,8 @@
     tm_src,
     tm_own,
     tr,
+    nb_src,
+    nb_in,
     s_ax,
     r_ax,
     s_rad,
@@ -66,6 +68,8 @@
     r_tm,
     s_tr,
     r_tr,
+    s_nb,
+    r_nb,
     ready,
     state,
     speed,
@@ -114,13 +118,17 @@
     def distances(pairs):
         return [(d, [r for r, x in pairs if x - r == d]) for d in sorted({x - r for r, x in pairs})]
 
+    around = [lax.rem(ax + axes - 1, axes), ax, lax.rem(ax + 1, axes)]
+
     @pl.when(rad > 0)
     def _():
-        greet({"rad": rad - 1})
+        for where in around:
+            greet({"rad": rad - 1, "ax": where})
 
     @pl.when(rad < rads - 1)
     def _():
-        greet({"rad": rad + 1})
+        for where in around:
+            greet({"rad": rad + 1, "ax": where})
 
     for d, senders in distances(own_pairs + sum_pairs):
 
@@ -138,14 +146,14 @@
         for k, pairs in enumerate(
             (
                 (
+                    (state_h.at[pl.ds(SV, 2)], state.at[pl.ds(SV, 2)]),
+                    (speed_h, speed),
+                    (visc_h, visc),
                     (area_h, area),
                     (station_h, station),
-                    (state_h.at[pl.ds(SV, 2)], state.at[pl.ds(SV, 2)]),
+                    (flags_h, flags),
                 ),
                 (
-                    (flags_h, flags),
-                    (speed_h, speed),
-                    (visc_h, visc),
                     (relax_h, relax),
                     (inlet_h, inlet),
                     (state_h.at[pl.ds(0, SV)], state.at[pl.ds(0, SV)]),
@@ -161,11 +169,13 @@
     def _():
         radr[:, 0] = jnp.zeros_like(radr[:, 0])
         tr[:, 0] = jnp.zeros_like(tr[:, 0])
+        nb_in[0] = jnp.zeros_like(nb_in[0])
 
     @pl.when(rad == rads - 1)
     def _():
         radr[:, 1] = jnp.zeros_like(radr[:, 1])
         tr[:, 1] = jnp.zeros_like(tr[:, 1])
+        nb_in[2] = jnp.zeros_like(nb_in[2])
 
     for d in range(1, DIRECT + 1):
 
@@ -188,7 +198,7 @@
         for _, x in own_pairs + sum_pairs:
             fixed[x] += 1
         for x in range(rads):
-            fixed[x] += (x > 0) + (x < rads - 1)
+            fixed[x] += 3 * (x > 0) + 3 * (x < rads - 1)
         pl.semaphore_wait(barrier, (axes - 1) + table(fixed) + jnp.where(row < rows - 1, axes, 0))
         for which, pairs in enumerate((own_pairs, sum_pairs)):
             for d, senders in distances(pairs):
@@ -208,22 +218,24 @@
 
     last = SWEEPS
 
-    group = lax.rem(lane, 64) // TX
-    half = lane // 64
+    group = lane // TX
     spot = lax.rem(lane, TX)
-
-    def tail_pack(rows_of, both):
+    middle = (group >= 4) & (group < 12)
+
+    def doubled(x):
+        return jnp.where(middle, x, pltpu.roll(x, 64, 1))
+
+    def tail_pack(row_of):
         acc = zero
         for r in range(RC):
-            for h in range(1 if both else 2):
-                moved = pltpu.roll(rows_of(h, r), (TX * (r + 1) + 64 * h) % NX, 1)
-                acc = jnp.where((group == r) & (half == h), moved, acc)
-        if both:
-            acc = jnp.where(half == 0, acc, pltpu.roll(acc, 64, 1))
-        return acc
+            acc = jnp.where(group == r + 4, pltpu.roll(row_of(r), (TX * (r + 5)) % NX, 1), acc)
+        return doubled(acc)
+
+    def wide(p):
+        return 2 * RC if p in (2, 3) else RC
 
     def tail_copy(p, d):
-        n = 2 * RC if p < last else RC
+        n = wide(p)
         return remote(
             tm_src.at[p, pl.ds(0, n)],
             tm_own.at[p, ax, pl.ds(0, n)],
@@ -233,8 +245,7 @@
         )
 
     def tail_all(p):
-        n = 2 * RC if p < last else RC
-        part = tm_own.at[p, pl.ds(0, axes - 1), pl.ds(0, n)]
+        part = tm_own.at[p, pl.ds(0, axes - 1), pl.ds(0, wide(p))]
         return remote(part, part, s_tm.at[p], r_tm.at[p], {"ax": ax})
 
     def tail_rad(p, up):
@@ -243,6 +254,30 @@
         return remote(
             tm_src.at[p, pl.ds(RC, RC)], tr.at[p, side], s_tr.at[p, side], r_tr.at[p, side], where
         )
+
+    def near_copy(i, j):
+        n = 3 * i + j
+        where = {"rad": rad + 1 - i, "ax": around[2 - j]}
+        return remote(nb_src, nb_in.at[i, j], s_nb.at[n], r_nb.at[n], where)
+
+    def near_each(action, sent):
+        for j in (1, 0, 2):
+            for i in (1, 0, 2):
+                if i == 1 and j == 1:
+                    continue
+                if i == 1:
+                    action(near_copy(i, j))
+                elif (i == 0) == sent:
+
+                    @pl.when(rad < rads - 1)
+                    def _():
+                        action(near_copy(i, j))
+
+                else:
+
+                    @pl.when(rad > 0)
+                    def _():
+                        action(near_copy(i, j))
 
     def total_copy(k, d):
         return remote(t_src.at[k, 0], px.at[k, d - 1], s_px.at[k, d - 1], r_px.at[k, d - 1], {"rad": rad + d})
@@ -266,22 +301,29 @@
         hot[r] = st
         for s in range(RC):
             weight[s, r] = jnp.where(st == float(s), ar, 0.0)
-        mine = group == r
+        mine = group == r + 4
         tail_station = jnp.where(mine, st, tail_station)
-        tail_area = jnp.where(mine & ((spot == TX - 1) | ((spot == TX - 2) & (half == 0))), ar, tail_area)
-    counted = (spot == TX - 2) & (half == 0)
-
-    def tail_send(p, q):
-        q = jnp.where(counted, 1.0, q)
+        tail_area = jnp.where(mine & (spot >= TX - 3), ar, tail_area)
+
+    def tail_sums(last_one, middle_one, first_one):
+        q = jnp.where(spot == TX - 1, last_one, zero)
+        q = jnp.where(spot == TX - 2, middle_one, q)
+        q = jnp.where(spot == TX - 3, first_one, q)
         total = zero
         for s in range(RC):
             part = jnp.sum(jnp.where(tail_station == float(s), tail_area, 0.0) * q, axis=0, keepdims=True)
             total = jnp.where(sub == s, part, total)
+        return total
+
+    def back(x, by):
+        return pltpu.roll(x, NX - by, 1)
+
+    def tail_send(p, total):
         tm_src[p, 0:RC] = total
         tm_own[p, ax, 0:RC] = total
         for d in range(1, axes):
             tail_copy(p, d).start()
-        if p < last:
+        if wide(p) > RC:
 
             @pl.when(rad > 0)
             def _():
@@ -310,10 +352,28 @@
     def at(x, i):
         return jnp.broadcast_to(x[:, i : i + 1], (8, NX))
 
-    tail = tail_pack(lambda h, r: state[SV + h, r], False)
-    tm_src[0, RC:] = tail
+    flag = flags[...].astype(jnp.float32)
+    tail_flag = zero
+    for r in range(RC):
+        fl = 0.5 * column(flag, r)
+        tail_flag = jnp.where(group == r + 4, fl, tail_flag)
+        a = 0.5 * speed[r]
+        coef[0, r] = a
+        coef[1, r] = a * fl
+        coef[2, r] = 0.5 * visc[r]
+    tails = [
+        tail_pack(lambda r: state[SV, r]),
+        tail_pack(lambda r: state[PV, r]),
+        tail_pack(lambda r: coef[0, r]),
+        tail_pack(lambda r: coef[2, r]),
+        doubled(tail_flag),
+    ]
+    for i, x in enumerate(tails):
+        nb_src[i] = x
     greeted()
-    tail_send(0, tail)
+    tail_send(0, tail_sums(tails[0], 1.0, back(tails[1], 2)))
+    near_each(lambda copy: copy.start(), True)
+    tail = tails[1]
 
     def sums(picks, p):
         total = zero
@@ -389,22 +449,52 @@
         lap = (f - b) + (rm + rp) + (cm + cp) - 4.0 * q
         return q * keep + (flux_in - g) + nu * lap
 
-    def tail_update(p, q, ghost):
-        left = tm_own[p, lax.rem(ax + axes - 1, axes), 2 * RC - 1 : 2 * RC]
-        right = tm_own[p, lax.rem(ax + 1, axes), RC : RC + 1]
-        a, ah, nu, keep = tail_coefs
+    def tail_step(q, lower, upper, cm, cp, coefs, keep, edge):
+        a, ah, nu = coefs
         b = q - pltpu.roll(q, 1, 1)
-        edge = 0.0 if ghost is None else jnp.where(half == 0, 0.0, ghost - q)
-        f = jnp.where(spot == TX - 1, edge, pltpu.roll(b, NX - 1, 1))
+        f = jnp.where(spot == TX - 1, edge, back(b, 1))
         slope = jnp.maximum(jnp.minimum(b, f), 0.0) + jnp.minimum(jnp.maximum(b, f), 0.0)
         g = a * q + ah * slope
-        rm = jnp.where(group == 0, pltpu.roll(tr[p, 0], 72, 1), pltpu.roll(q, TX, 1))
-        rp = jnp.where(group == RC - 1, pltpu.roll(tr[p, 1], 56, 1), pltpu.roll(q, NX - TX, 1))
-        cm = jnp.where(sub == 0, left, pltpu.roll(q, 1, 0))
-        cp = jnp.where(sub == CC - 1, right, pltpu.roll(q, CC - 1, 0))
-        lap = (f - b) + (rm + rp) + (cm + cp) - 4.0 * q
-        new = q * keep + (pltpu.roll(g, 1, 1) - g) + nu * lap
-        return jnp.where(half == 0, new, q) if ghost is None else new
+        lap = (f - b) + (lower + upper) + (cm + cp) - 4.0 * q
+        return q * keep + (pltpu.roll(g, 1, 1) - g) + nu * lap
+
+    def tail_update(p, q, ghost):
+        if p == 1:
+            lo, hi, left, right = [nb_in[i, j, 1] for i, j in ((0, 1), (2, 1), (1, 0), (1, 2))]
+        else:
+            lo, hi = tr[p, 0], tr[p, 1]
+            left, right = [tm_own[p, around[j], RC : 2 * RC] for j in (0, 2)]
+        full = jnp.where(group < 4, lo, jnp.where(group < 12, q, hi))
+        cm = jnp.where(sub == 0, left[CC - 1 : CC], pltpu.roll(q, 1, 0))
+        cp = jnp.where(sub == CC - 1, right[0:1], pltpu.roll(q, CC - 1, 0))
+        coefs = (tails[2], tails[2] * tails[4], tails[3])
+        keep = 1.0 - 0.5 * relax[PV]
+        new = tail_step(q, pltpu.roll(full, TX, 1), back(full, TX), cm, cp, coefs, keep, ghost - q)
+        return doubled(new)
+
+    def deep(i):
+        def comb(j):
+            own = tails[i] if j == 1 else nb_in[1, j, i]
+            return jnp.where(group < 4, nb_in[0, j, i], jnp.where(group < 12, own, nb_in[2, j, i]))
+
+        return comb(1), jnp.where(sub < 4, comb(2), comb(0))
+
+    def deep_sections():
+        pair = deep(0)
+        a, nu, fl = deep(2), deep(3), deep(4)
+        keep = 1.0 - 0.5 * relax[SV]
+        found = []
+        for _ in range(SWEEPS - 1):
+            new = []
+            for h in range(2):
+                q, other = pair[h], pair[1 - h]
+                cm = jnp.where(sub == 0, other[CC - 1 : CC], pltpu.roll(q, 1, 0))
+                cp = jnp.where(sub == CC - 1, other[0:1], pltpu.roll(q, CC - 1, 0))
+                coefs = (a[h], a[h] * fl[h], nu[h])
+                new.append(tail_step(q, pltpu.roll(q, TX, 1), back(q, TX), cm, cp, coefs, keep, 0.0))
+            pair = new
+            found.append(pair[0])
+        return found
 
     def sweep(p, v, src, dst, pressures):
         keep = 1.0 - 0.5 * relax[v]
@@ -433,23 +523,8 @@
     sums(lax.fori_loop(0, NV, first, (one,) * RC), 0)
     field_send(0)
 
-    flag = flags[...].astype(jnp.float32)
-    tail_flag = zero
     for r in range(RC):
-        fl = 0.5 * column(flag, r)
-        tail_flag = jnp.where(group == r, fl, tail_flag)
-        a = 0.5 * speed[r]
-        coef[0, r] = a
-        coef[1, r] = a * fl
-        coef[2, r] = 0.5 * visc[r]
         field[0, PV, r] = state[PV, r]
-    tail_a = tail_pack(lambda h, r: coef[0, r], True)
-    tail_coefs = (
-        tail_a,
-        tail_a * tail_flag,
-        tail_pack(lambda h, r: coef[2, r], True),
-        1.0 - 0.5 * jnp.where(half == 0, relax[SV], relax[PV]),
-    )
     turned = zero
     inlet_all = inlet[...]
     for v in range(NV):
@@ -459,7 +534,7 @@
 
     def write_profile(v, wide):
         line = jnp.sum(jnp.where(diagonal, wide, 0.0), axis=0, keepdims=True)
-        out_profile[v : v + 1, :] = line[:, :RC]
+        out_profile[v] = line[:, :RC]
 
     def total_of(load):
         total = load(0)
@@ -467,71 +542,91 @@
             total = total + load(d)
         return total
 
-    swirl = None
+    def send_totals(batch):
+        for k in batch:
+            for d, senders in own_steps:
+
+                @pl.when(among(senders))
+                def _():
+                    total_copy(k, d).start()
+
+    def totals_in(batch):
+        for k in batch:
+            for d, senders in own_steps:
+
+                @pl.when(among([r + d for r in senders]))
+                def _():
+                    total_copy(k, d).wait_recv()
+
+            @pl.when(among([x for x in range(rads) if BASE[x] >= 0]))
+            def _():
+                sum_copy(k, 1).wait_recv()
+
+        before = []
+        for k in batch:
+            before.append(jnp.sum(px[k], axis=0))
+            t_src[k, 1] = before[-1] + t_src[k, 0]
+        if batch[0] == 0:
+            await_ready(1)
+        for d, senders in sum_steps:
+
+            @pl.when(among(senders))
+            def _():
+                for k in batch:
+                    sum_copy(k, d).start()
+
+        return before
+
+    scale = 4.0 / (RC * rads)
+    swirls, befores = [], []
+
+    def add_swirl(third):
+        swirls.append(third * third / radius)
+        t_src[len(swirls) - 1, 0] = jnp.sum(swirls[-1], axis=0, keepdims=True)
+
     for p in range(SWEEPS + 1):
         tail_all(p).wait_recv()
-        if p < last:
-
-            @pl.when(rad > 0)
-            def _():
-                tail_rad(p, True).wait_recv()
-
-            @pl.when(rad < rads - 1)
-            def _():
-                tail_rad(p, False).wait_recv()
-
         folded = fold(total_of(lambda d: tm_own[p, d, 0:RC]))
-        areas_in = at(folded, 62)
-        ghost = None
-        if p >= 1:
-            for d, senders in own_steps:
-
-                @pl.when(among([r + d for r in senders]))
+        if p == 0:
+            areas_in = at(folded, 94)
+            fourth = at(folded, 93) / areas_in
+            add_swirl(at(folded, 95) / areas_in)
+            await_ready(0)
+            send_totals((0,))
+            near_each(lambda copy: copy.wait_recv(), False)
+            one_on, two_on, three_on = deep_sections()
+            tail_send(1, tail_sums(one_on, back(two_on, 1), back(three_on, 2)))
+        else:
+            if p == 1:
+                for i in (95, 94, 93):
+                    add_swirl(at(folded, i) / areas_in)
+                send_totals((1, 2, 3))
+            else:
+                fourth = at(folded, 95) / areas_in
+            if wide(p) > RC:
+
+                @pl.when(rad > 0)
                 def _():
-                    total_copy(p - 1, d).wait_recv()
-
-            @pl.when(among([x for x in range(rads) if BASE[x] >= 0]))
-            def _():
-                sum_copy(p - 1, 1).wait_recv()
-
-            before = jnp.sum(px[p - 1], axis=0)
-            t_src[p - 1, 1] = before + t_src[p - 1, 0]
-            if p == 1:
-                await_ready(1)
-            for d, senders in sum_steps:
-
-                @pl.when(among(senders))
+                    tail_rad(p, True).wait_recv()
+
+                @pl.when(rad < rads - 1)
                 def _():
-                    sum_copy(p - 1, d).start()
-
-            run = swirl
+                    tail_rad(p, False).wait_recv()
+
+            run = swirls[p - 1]
             for step in (1, 2, 4):
                 run = run + jnp.where(sub >= step, pltpu.roll(run, step, 0), 0.0)
-            scale = 4.0 / (RC * rads)
-            fourth = at(folded, 127) / areas_in
-            pressure = fourth + scale * ((run - swirl) + before)
+            pressure = fourth + scale * ((run - swirls[p - 1]) + befores[p - 1])
             profile_s[...] = pressure
             rows_of = [profile_s[s : s + 1, :] for s in range(RC)]
             if p < last:
                 ghost = jnp.broadcast_to(rows_of[0], (8, NX))
                 for s in range(1, RC):
                     ghost = jnp.where(tail_station == float(s), rows_of[s], ghost)
-        if p < last:
-            third = at(folded, 63) / areas_in
-            swirl = third * third / radius
-            t_src[p, 0] = jnp.sum(swirl, axis=0, keepdims=True)
-            tail = tail_update(p, tail, ghost)
-            if p + 1 < last:
-                tm_src[p + 1, RC:] = tail
-            tail_send(p + 1, tail)
-
-            if p == 0:
-                await_ready(0)
-            for d, senders in own_steps:
-
-                @pl.when(among(senders))
-                def _():
-                    total_copy(p, d).start()
+                tail = tail_update(p, tail, ghost)
+                if wide(p + 1) > RC:
+                    tm_src[p + 1, RC:] = tail
+                tail_send(p + 1, tail_sums(tail, 1.0, zero))
 
         src = of(p)
 
@@ -545,7 +640,7 @@
             total = total_of(lambda d: ms_up[p, d])
             if p == last:
                 total = fold(total)
-                upstream[...] = at(total, 127) / at(total, 62)
+                upstream[...] = at(total, 95) / at(total, 94)
             else:
                 upstream[...] = total / at(total, NV)
 
@@ -597,6 +692,10 @@
             if p + 1 < SWEEPS:
                 sums(tuple(jnp.where(lane == PV, at(fresh[r], NX - 1), picks[r]) for r in range(RC)), p + 1)
             field_send(p + 1)
+        if p == 0:
+            befores += totals_in((0,))
+        if p == 1:
+            befores += totals_in((1, 2, 3))
 
     remote(ms_own.at[pl.ds(0, axes - 1)], ms_own.at[pl.ds(0, axes - 1)], s_own, r_own, {"ax": ax}).wait_recv()
     total = total_of(lambda d: ms_own[d])
@@ -605,6 +704,7 @@
         write_profile(v, fourth if v == PV else at(profile, v))
     out_pressure[...] = jnp.sum(jnp.where(diagonal, pressure, 0.0), axis=0, keepdims=True)[:, :RC]
 
+    near_each(lambda copy: copy.wait_send(), True)
     remote(ms_own.at[pl.ds(0, axes - 1)], ms_own.at[pl.ds(0, axes - 1)], s_own, r_own, {"ax": ax}).wait_send()
     for p in range(SWEEPS + 1):
         tail_all(p).wait_send()
@@ -616,13 +716,13 @@
         @pl.when(rad < rads - 1)
         def _():
             rad_copy(p, True).wait_send()
-            if p < last:
+            if wide(p) > RC:
                 tail_rad(p, True).wait_send()
 
         @pl.when(rad > 0)
         def _():
             rad_copy(p, False).wait_send()
-            if p < last:
+            if wide(p) > RC:
                 tail_rad(p, False).wait_send()
 
         ax_copy(p, True).wait_send()
@@ -639,6 +739,17 @@
                 @pl.when(among(senders))
                 def _():
                     sum_copy(p, d).wait_send()
+
+
+def store(new, profile, pressure, out, out_profile, out_pressure, sems):
+    copies = [
+        pltpu.make_async_copy(src, dst, sems.at[i])
+        for i, (src, dst) in enumerate(((new, out), (profile, out_profile), (pressure, out_pressure)))
+    ]
+    for copy in copies:
+        copy.start()
+    for copy in copies:
+        copy.wait()
 
 
 def solution(mesh):
@@ -655,7 +766,7 @@
             functools.partial(kernel, sizes),
             out_shape=(
                 jax.ShapeDtypeStruct((NV, RC, CC, NX), f32),
-                jax.ShapeDtypeStruct((NV, RC), f32),
+                jax.ShapeDtypeStruct((NV, 1, RC), f32),
                 jax.ShapeDtypeStruct((1, RC), f32),
             ),
             in_specs=[hbm] * 8,
@@ -680,6 +791,8 @@
                 pltpu.VMEM((phases, 2 * RC, NX), f32),
                 pltpu.VMEM((phases, axes, 2 * RC, NX), f32),
                 pltpu.VMEM((SWEEPS, 2, CC, NX), f32),
+                pltpu.VMEM((5, CC, NX), f32),
+                pltpu.VMEM((3, 3, 5, CC, NX), f32),
                 dma((phases, 2)),
                 dma((phases, 2)),
                 dma((phases, 2)),
@@ -694,6 +807,8 @@
                 dma((phases,)),
                 dma((SWEEPS, 2)),
                 dma((SWEEPS, 2)),
+                dma((9,)),
+                dma((9,)),
                 pltpu.SemaphoreType.REGULAR((2,)),
                 pltpu.VMEM((NV, RC, CC, NX), f32),
                 pltpu.VMEM((RC, CC, NX), f32),
@@ -723,7 +838,19 @@
                 )
             ]
         )
-        return new[:, None], profile[:, None], pressure
+        new, profile, pressure = pl.pallas_call(
+            store,
+            out_shape=(
+                jax.ShapeDtypeStruct((NV, RC, CC, NX), f32),
+                jax.ShapeDtypeStruct((NV, 1, RC), f32),
+                jax.ShapeDtypeStruct((1, RC), f32),
+            ),
+            in_specs=[vmem] * 3,
+            out_specs=(hbm,) * 3,
+            scratch_shapes=[dma((3,))],
+            compiler_params=pltpu.CompilerParams(vmem_limit_bytes=4 * 1024 * 1024),
+        )(new, profile, pressure)
+        return new[:, None], profile, pressure
 
     return jax.shard_map(
         body,

time: 41.1 us -> 38.5 us (0.937)
  local copies, waits for them, and re-layouts: 1.78 us -> 0 us
  Pallas kernels: 38.6 us -> 37.8 us
    unnamed x3 -> x0, local copies, waits for them, and re-layouts: 1.78 us -> none
    pallas_call x1, Pallas kernels: 38.6 us -> 37 us  [body(): pl.pallas_call(functools.partial(kernel, sizes), out_shape=(jax.ShapeDtyp...]
    pallas_call x0 -> x1, Pallas kernels: none -> 0.72 us  [body(): pl.pallas_call(store, out_shape=(jax.ShapeDtypeStruct((NV, RC, CC, NX), f...]
where the time goes in v3:
time: 38.5 us; the launch traced here: 38.4 us
  Pallas kernels  37.8 us (98%)
  between operations  0.64 us (2%)
    pallas_call x1, Pallas kernels, body(): pl.pallas_call(functools.partial(kernel, sizes), out_shape=(jax.ShapeDtyp...  37 us

profile of v3, /device:TPU:483, one launch (start us, length us, event | category | flops | bytes accessed | tf_op | source)
XLA Modules:
  0.0 38.4 jit_solution(7771400228068143071)
XLA Ops:
  0.6 37.0 %shard_map.103 = (f32[7,8,8,128]{3,2,1,0:T(8,128)S(1)}, f32[7,1,8]{2,1,0:T(1,128)S(1)}, f32[1,8]{1,0:T(1,128)S(1)}) custom-call(f32[7,8,8,128]{3,2,1,0:T(8,128)} %bitcast.9, f32[8,8,128]{2,1,0:T(8,128)} %bitcast.10, f32[8,8,128]{2,1,0:T(8,128)} %bitcast.11, f32[7]{0:T(128)} %relax_h.1, f32[8,8]{1,0:T(8,128)} %bitcast.12, s32[8,8]{1,0:T(8,128)} %bitcast.13, ...), custom_call_target="tpu_custom_call" | custom-call | tf_op jit(solution)/shard_map/pallas_call | solution.py:765
  37.7 0.7 %shard_map.104 = (f32[7,8,8,128]{3,2,1,0:T(8,128)}, f32[7,1,8]{2,1,0:T(1,128)}, f32[1,8]{1,0:T(1,128)}) custom-call(f32[7,8,8,128]{3,2,1,0:T(8,128)S(1)} %get-tuple-element.9.new, f32[7,1,8]{2,1,0:T(1,128)S(1)} %get-tuple-element.10.profile, f32[1,8]{1,0:T(1,128)S(1)} %get-tuple-element.11.pressure), custom_call_target="tpu_custom_call" | custom-call | tf_op jit(solution)/shard_map/pallas_call | solution.py:841

commit v4 on v3

--- a/solution.py
+++ b/solution.py
@@ -116,7 +116,7 @@
         return (lax.shift_right_logical(jnp.int32(mask), rad) & 1) == 1
 
     def distances(pairs):
-        return [(d, [r for r, x in pairs if x - r == d]) for d in sorted({x - r for r, x in pairs})]
+        return [(d, [r for r, x in pairs if x - r == d]) for d in sorted({x - r for r, x in pairs}, reverse=True)]
 
     around = [lax.rem(ax + axes - 1, axes), ax, lax.rem(ax + 1, axes)]
 
@@ -193,6 +193,8 @@
         wide = jnp.broadcast_to(ref[r : r + 1, :], (8, 8))
         return jnp.broadcast_to(jnp.sum(jnp.where(diagonal[:, :8], wide, 0.0), axis=1, keepdims=True), (8, NX))
 
+    partners = sorted(range(1, axes), key=lambda d: (-min(d, axes - d), d))
+
     def greeted():
         fixed = [0] * rads
         for _, x in own_pairs + sum_pairs:
@@ -261,8 +263,8 @@
         return remote(nb_src, nb_in.at[i, j], s_nb.at[n], r_nb.at[n], where)
 
     def near_each(action, sent):
-        for j in (1, 0, 2):
-            for i in (1, 0, 2):
+        for j in (0, 2, 1):
+            for i in (0, 2, 1):
                 if i == 1 and j == 1:
                     continue
                 if i == 1:
@@ -321,7 +323,7 @@
     def tail_send(p, total):
         tm_src[p, 0:RC] = total
         tm_own[p, ax, 0:RC] = total
-        for d in range(1, axes):
+        for d in partners:
             tail_copy(p, d).start()
         if wide(p) > RC:
 
@@ -337,12 +339,12 @@
 
             @pl.when(row < rows - 1)
             def _():
-                for d in range(axes):
+                for d in partners + [0]:
                     up_copy(p, d).start()
 
     def up_copy(p, d):
         src = tm_src.at[p, pl.ds(0, RC)] if p == last else ms_src.at[p]
-        return remote(src, ms_up.at[p, ax], s_down.at[p], r_up.at[p], {"row": row + 1, "ax": d})
+        return remote(src, ms_up.at[p, ax], s_down.at[p], r_up.at[p], {"row": row + 1, "ax": lax.rem(ax + d, axes)})
 
     def fold(total):
         for step in (8, 16, 32):
@@ -419,7 +421,7 @@
 
             @pl.when(row < rows - 1)
             def _():
-                for d in range(axes):
+                for d in partners + [0]:
                     up_copy(p, d).start()
 
         @pl.when(rad < rads - 1)
@@ -433,7 +435,7 @@
         ax_copy(p, True).start()
         ax_copy(p, False).start()
         if p == last - 1:
-            for d in range(1, axes):
+            for d in partners:
                 own_copy(d).start()
 
     def update(q, rm, rp, left, right, coefs, ghost, edge, keep):
@@ -584,7 +586,55 @@
         swirls.append(third * third / radius)
         t_src[len(swirls) - 1, 0] = jnp.sum(swirls[-1], axis=0, keepdims=True)
 
+    def sent(p):
+        tail_all(p).wait_send()
+
+        @pl.when(row < rows - 1)
+        def _():
+            remote(ms_up.at[p], ms_up.at[p], s_down.at[p], r_up.at[p], {"ax": ax}).wait_send()
+
+        @pl.when(rad < rads - 1)
+        def _():
+            rad_copy(p, True).wait_send()
+            if wide(p) > RC:
+                tail_rad(p, True).wait_send()
+
+        @pl.when(rad > 0)
+        def _():
+            rad_copy(p, False).wait_send()
+            if wide(p) > RC:
+                tail_rad(p, False).wait_send()
+
+        ax_copy(p, True).wait_send()
+        ax_copy(p, False).wait_send()
+
+    def totals_sent(k):
+        for d, senders in own_steps:
+
+            @pl.when(among(senders))
+            def _():
+                total_copy(k, d).wait_send()
+
+        for d, senders in sum_steps:
+
+            @pl.when(among(senders))
+            def _():
+                sum_copy(k, d).wait_send()
+
+    own_part = ms_own.at[pl.ds(0, axes - 1)]
+    own_all = remote(own_part, own_part, s_own, r_own, {"ax": ax})
+
     for p in range(SWEEPS + 1):
+        if p == last:
+            own_all.wait_recv()
+            total = total_of(lambda d: ms_own[d])
+            profile = total / at(total, NV)
+            for v in range(NV):
+                if v != PV:
+                    write_profile(v, at(profile, v))
+            own_all.wait_send()
+            sent(p - 1)
+
         tail_all(p).wait_recv()
         folded = fold(total_of(lambda d: tm_own[p, d, 0:RC]))
         if p == 0:
@@ -696,49 +746,19 @@
             befores += totals_in((0,))
         if p == 1:
             befores += totals_in((1, 2, 3))
-
-    remote(ms_own.at[pl.ds(0, axes - 1)], ms_own.at[pl.ds(0, axes - 1)], s_own, r_own, {"ax": ax}).wait_recv()
-    total = total_of(lambda d: ms_own[d])
-    profile = total / at(total, NV)
-    for v in range(NV):
-        write_profile(v, fourth if v == PV else at(profile, v))
+            near_each(lambda copy: copy.wait_send(), True)
+        if 1 <= p < last:
+            sent(p - 1)
+        if p == 2:
+            totals_sent(0)
+            totals_sent(1)
+        if p == 3:
+            totals_sent(2)
+            totals_sent(3)
+
+    write_profile(PV, fourth)
     out_pressure[...] = jnp.sum(jnp.where(diagonal, pressure, 0.0), axis=0, keepdims=True)[:, :RC]
-
-    near_each(lambda copy: copy.wait_send(), True)
-    remote(ms_own.at[pl.ds(0, axes - 1)], ms_own.at[pl.ds(0, axes - 1)], s_own, r_own, {"ax": ax}).wait_send()
-    for p in range(SWEEPS + 1):
-        tail_all(p).wait_send()
-
-        @pl.when(row < rows - 1)
-        def _():
-            remote(ms_up.at[p], ms_up.at[p], s_down.at[p], r_up.at[p], {"ax": ax}).wait_send()
-
-        @pl.when(rad < rads - 1)
-        def _():
-            rad_copy(p, True).wait_send()
-            if wide(p) > RC:
-                tail_rad(p, True).wait_send()
-
-        @pl.when(rad > 0)
-        def _():
-            rad_copy(p, False).wait_send()
-            if wide(p) > RC:
-                tail_rad(p, False).wait_send()
-
-        ax_copy(p, True).wait_send()
-        ax_copy(p, False).wait_send()
-        if p < last:
-            for d, senders in own_steps:
-
-                @pl.when(among(senders))
-                def _():
-                    total_copy(p, d).wait_send()
-
-            for d, senders in sum_steps:
-
-                @pl.when(among(senders))
-                def _():
-                    sum_copy(p, d).wait_send()
+    sent(last)
 
 
 def store(new, profile, pressure, out, out_profile, out_pressure, sems):

time: 38.5 us -> 38 us (0.987)
  Pallas kernels: 37.8 us -> 37.2 us
    pallas_call x1, Pallas kernels: 37 us -> 36.5 us  [body(): pl.pallas_call(functools.partial(kernel, sizes), out_shape=(jax.ShapeDtyp...]
where the time goes in v4:
time: 38 us; the launch traced here: 37.8 us
  Pallas kernels  37.2 us (98%)
  between operations  0.64 us (2%)
    pallas_call x1, Pallas kernels, body(): pl.pallas_call(functools.partial(kernel, sizes), out_shape=(jax.ShapeDtyp...  36.5 us

profile of v4, /device:TPU:483, one launch (start us, length us, event | category | flops | bytes accessed | tf_op | source)
XLA Modules:
  0.0 37.8 jit_solution(15780257326461482446)
XLA Ops:
  0.6 36.5 %shard_map.103 = (f32[7,8,8,128]{3,2,1,0:T(8,128)S(1)}, f32[7,1,8]{2,1,0:T(1,128)S(1)}, f32[1,8]{1,0:T(1,128)S(1)}) custom-call(f32[7,8,8,128]{3,2,1,0:T(8,128)} %bitcast.9, f32[8,8,128]{2,1,0:T(8,128)} %bitcast.10, f32[8,8,128]{2,1,0:T(8,128)} %bitcast.11, f32[7]{0:T(128)} %relax_h.1, f32[8,8]{1,0:T(8,128)} %bitcast.12, s32[8,8]{1,0:T(8,128)} %bitcast.13, ...), custom_call_target="tpu_custom_call" | custom-call | tf_op jit(solution)/shard_map/pallas_call | solution.py:785
  37.1 0.7 %shard_map.104 = (f32[7,8,8,128]{3,2,1,0:T(8,128)}, f32[7,1,8]{2,1,0:T(1,128)}, f32[1,8]{1,0:T(1,128)}) custom-call(f32[7,8,8,128]{3,2,1,0:T(8,128)S(1)} %get-tuple-element.9.new, f32[7,1,8]{2,1,0:T(1,128)S(1)} %get-tuple-element.10.profile, f32[1,8]{1,0:T(1,128)S(1)} %get-tuple-element.11.pressure), custom_call_target="tpu_custom_call" | custom-call | tf_op jit(solution)/shard_map/pallas_call | solution.py:861

commit v5 on v4

--- a/solution.py
+++ b/solution.py
@@ -181,11 +181,11 @@
 
         @pl.when(jnp.logical_not(among([x for x in range(rads) if x - d in heard[x]])))
         def _():
-            px[:, d - 1] = jnp.zeros_like(px[:, d - 1])
+            px[d - 1] = jnp.zeros_like(px[d - 1])
 
     @pl.when(among([x for x in range(rads) if BASE[x] < 0]))
     def _():
-        px[:, DIRECT] = jnp.zeros_like(px[:, DIRECT])
+        px[DIRECT] = jnp.zeros_like(px[DIRECT])
 
     diagonal = sub == lane
 
@@ -282,11 +282,13 @@
                         action(near_copy(i, j))
 
     def total_copy(k, d):
-        return remote(t_src.at[k, 0], px.at[k, d - 1], s_px.at[k, d - 1], r_px.at[k, d - 1], {"rad": rad + d})
+        part = pl.ds(0, 1) if k == 0 else pl.ds(1, SWEEPS - 1)
+        return remote(t_src.at[0, part], px.at[d - 1, part], s_px.at[k, d - 1], r_px.at[k, d - 1], {"rad": rad + d})
 
     def sum_copy(k, d):
         where = {"rad": rad + d}
-        return remote(t_src.at[k, 1], px.at[k, DIRECT], s_px.at[k, DIRECT + d - 1], r_px.at[k, DIRECT], where)
+        part = pl.ds(0, 1) if k == 0 else pl.ds(1, SWEEPS - 1)
+        return remote(t_src.at[1, part], px.at[DIRECT, part], s_px.at[k, DIRECT + d - 1], r_px.at[k, DIRECT], where)
 
     own_steps = distances(own_pairs + [(x - 1, x) for x in range(1, rads)])
     sum_steps = distances(sum_pairs)
@@ -544,38 +546,35 @@
             total = total + load(d)
         return total
 
-    def send_totals(batch):
-        for k in batch:
-            for d, senders in own_steps:
-
-                @pl.when(among(senders))
-                def _():
-                    total_copy(k, d).start()
-
-    def totals_in(batch):
-        for k in batch:
-            for d, senders in own_steps:
-
-                @pl.when(among([r + d for r in senders]))
-                def _():
-                    total_copy(k, d).wait_recv()
-
-            @pl.when(among([x for x in range(rads) if BASE[x] >= 0]))
+    def send_totals(k):
+        for d, senders in own_steps:
+
+            @pl.when(among(senders))
             def _():
-                sum_copy(k, 1).wait_recv()
+                total_copy(k, d).start()
+
+    def totals_in(k):
+        for d, senders in own_steps:
+
+            @pl.when(among([r + d for r in senders]))
+            def _():
+                total_copy(k, d).wait_recv()
+
+        @pl.when(among([x for x in range(rads) if BASE[x] >= 0]))
+        def _():
+            sum_copy(k, 1).wait_recv()
 
         before = []
-        for k in batch:
-            before.append(jnp.sum(px[k], axis=0))
-            t_src[k, 1] = before[-1] + t_src[k, 0]
-        if batch[0] == 0:
+        for i in range(1) if k == 0 else range(1, SWEEPS):
+            before.append(jnp.sum(px[:, i], axis=0))
+            t_src[1, i] = before[-1] + t_src[0, i]
+        if k == 0:
             await_ready(1)
         for d, senders in sum_steps:
 
             @pl.when(among(senders))
             def _():
-                for k in batch:
-                    sum_copy(k, d).start()
+                sum_copy(k, d).start()
 
         return before
 
@@ -584,7 +583,7 @@
 
     def add_swirl(third):
         swirls.append(third * third / radius)
-        t_src[len(swirls) - 1, 0] = jnp.sum(swirls[-1], axis=0, keepdims=True)
+        t_src[0, len(swirls) - 1] = jnp.sum(swirls[-1], axis=0, keepdims=True)
 
     def sent(p):
         tail_all(p).wait_send()
@@ -642,7 +641,7 @@
             fourth = at(folded, 93) / areas_in
             add_swirl(at(folded, 95) / areas_in)
             await_ready(0)
-            send_totals((0,))
+            send_totals(0)
             near_each(lambda copy: copy.wait_recv(), False)
             one_on, two_on, three_on = deep_sections()
             tail_send(1, tail_sums(one_on, back(two_on, 1), back(three_on, 2)))
@@ -650,7 +649,7 @@
             if p == 1:
                 for i in (95, 94, 93):
                     add_swirl(at(folded, i) / areas_in)
-                send_totals((1, 2, 3))
+                send_totals(1)
             else:
                 fourth = at(folded, 95) / areas_in
             if wide(p) > RC:
@@ -743,18 +742,16 @@
                 sums(tuple(jnp.where(lane == PV, at(fresh[r], NX - 1), picks[r]) for r in range(RC)), p + 1)
             field_send(p + 1)
         if p == 0:
-            befores += totals_in((0,))
+            befores += totals_in(0)
         if p == 1:
-            befores += totals_in((1, 2, 3))
+            befores += totals_in(1)
             near_each(lambda copy: copy.wait_send(), True)
         if 1 <= p < last:
             sent(p - 1)
         if p == 2:
             totals_sent(0)
+        if p == 3:
             totals_sent(1)
-        if p == 3:
-            totals_sent(2)
-            totals_sent(3)
 
     write_profile(PV, fourth)
     out_pressure[...] = jnp.sum(jnp.where(diagonal, pressure, 0.0), axis=0, keepdims=True)[:, :RC]
@@ -799,8 +796,8 @@
                 pltpu.VMEM((phases, RC, NX), f32),
                 pltpu.VMEM((axes, RC, NX), f32),
                 pltpu.VMEM((phases, axes, RC, NX), f32),
-                pltpu.VMEM((SWEEPS, 2, 1, NX), f32),
-                pltpu.VMEM((SWEEPS, DIRECT + 1, 1, NX), f32),
+                pltpu.VMEM((2, SWEEPS, 1, NX), f32),
+                pltpu.VMEM((DIRECT + 1, SWEEPS, 1, NX), f32),
                 pltpu.VMEM((3, RC, CC, NX), f32),
                 pltpu.VMEM((RC, RC, CC, NX), f32),
                 pltpu.VMEM((RC, CC, NX), f32),
@@ -821,8 +818,8 @@
                 dma,
                 dma((phases,)),
                 dma((phases,)),
-                dma((SWEEPS, 2 * DIRECT + 1)),
-                dma((SWEEPS, DIRECT + 1)),
+                dma((2, 2 * DIRECT + 1)),
+                dma((2, DIRECT + 1)),
                 dma((phases,)),
                 dma((phases,)),
                 dma((SWEEPS, 2)),

time: 38 us -> 37.3 us (0.982)
  Pallas kernels: 37.2 us -> 36.5 us
    pallas_call x1, Pallas kernels: 36.5 us -> 35.8 us  [body(): pl.pallas_call(functools.partial(kernel, sizes), out_shape=(jax.ShapeDtyp...]
where the time goes in v5:
time: 37.3 us; the launch traced here: 37.1 us
  Pallas kernels  36.5 us (98%)
  between operations  0.64 us (2%)
    pallas_call x1, Pallas kernels, body(): pl.pallas_call(functools.partial(kernel, sizes), out_shape=(jax.ShapeDtyp...  35.8 us

profile of v5, /device:TPU:483, one launch (start us, length us, event | category | flops | bytes accessed | tf_op | source)
XLA Modules:
  0.0 37.1 jit_solution(17604346158249336868)
XLA Ops:
  0.6 35.8 %shard_map.103 = (f32[7,8,8,128]{3,2,1,0:T(8,128)S(1)}, f32[7,1,8]{2,1,0:T(1,128)S(1)}, f32[1,8]{1,0:T(1,128)S(1)}) custom-call(f32[7,8,8,128]{3,2,1,0:T(8,128)} %bitcast.9, f32[8,8,128]{2,1,0:T(8,128)} %bitcast.10, f32[8,8,128]{2,1,0:T(8,128)} %bitcast.11, f32[7]{0:T(128)} %relax_h.1, f32[8,8]{1,0:T(8,128)} %bitcast.12, s32[8,8]{1,0:T(8,128)} %bitcast.13, ...), custom_call_target="tpu_custom_call" | custom-call | tf_op jit(solution)/shard_map/pallas_call | solution.py:782
  36.4 0.7 %shard_map.104 = (f32[7,8,8,128]{3,2,1,0:T(8,128)}, f32[7,1,8]{2,1,0:T(1,128)}, f32[1,8]{1,0:T(1,128)}) custom-call(f32[7,8,8,128]{3,2,1,0:T(8,128)S(1)} %get-tuple-element.9.new, f32[7,1,8]{2,1,0:T(1,128)S(1)} %get-tuple-element.10.profile, f32[1,8]{1,0:T(1,128)S(1)} %get-tuple-element.11.pressure), custom_call_target="tpu_custom_call" | custom-call | tf_op jit(solution)/shard_map/pallas_call | solution.py:858
